TPU v7x, 256 devices: a whole 4x4x8 slice. The times are simulated.
256 devices in a mesh: dp: 32 (over z, y_lo, core), replica: 8 (over x, y_hi).
Axes of the slice: x: 4, y: 4 (y_hi: 2, y_lo: 2; y = y_hi * 2 + y_lo), z: 8, core: 2. Of those that a mesh axis runs over, the one named last changes fastest.
Arguments:
- picture_encoder_features: bfloat16 [57344, 1152], P(('dp', 'replica')), may hold values from -24 to 24
- text_encoder_features: bfloat16 [57344, 1152], P(('dp', 'replica')), may hold values from -24 to 24
- picture_projector: bfloat16 [1152, 1152], replicated, may hold values from -0.1875 to 0.1875
- text_projector: bfloat16 [1152, 1152], replicated, may hold values from -0.1875 to 0.1875
- matching_target: int32 [57344], P(('dp', 'replica')), may hold values from 0 to 223, as said below
- sharpness_param: float32 [1], replicated, may hold values from 10 to 40
- offset_shift: float32 [1], replicated, may hold values from -4 to -1
- objective_multiplier: float32 [1], replicated, may hold values from 64 to 512
Outputs:
- grad_image_head: float32 [1152, 1152], P('dp')
- grad_caption_head: float32 [1152, 1152], P('dp')
Inputs may be any that keep to these rules, and one draw needn't show every extreme that they name: Within each device's 224 rows the entries are a permutation of 0 to 223: image row r of a block matches caption row matching_target[r] of the same block.
All inputs are finite; a program needn't handle non-finite values.
Results may differ from a plain program's by a relative error of at most 0.0025.
Values may be sent and summed in bfloat16 or wider, within the bound.
No kernel may reach another device: no remote copies, remote signals or barrier semaphores. Data moves between devices by JAX's collectives and lax.ppermute only.
A program may use at most 128 MiB of HBM per device.

v0:
```python
import jax
import jax.numpy as jnp
import numpy as np
from jax import lax
from jax.experimental import pallas as pl
from jax.experimental.pallas import tpu as pltpu
from jax.sharding import PartitionSpec as P

AXES = ("dp", "replica")
NX, NY, NZ = 4, 4, 8
R, D, PAD = 224, 1152, 256
F32, BF16 = jnp.float32, jnp.bfloat16


def device_at(x, y, z, core):
    x, y, z = x % NX, y % NY, z % NZ
    return (z * 4 + (y % 2) * 2 + core) * 8 + x * 2 + y // 2


PLACES = [(x, y, z, c) for x in range(NX) for y in range(NY) for z in range(NZ) for c in range(2)]


ALONG_Z = [[device_at(x, y, z, c) for z in range(NZ)] for x in range(NX) for y in range(NY) for c in range(2)]


def moved(value, to):
    pairs = []
    for place in PLACES:
        target = to(*place)
        if target is not None:
            pairs.append((device_at(*place), device_at(*target)))
    return lax.ppermute(value, AXES, pairs)


def swap_cores(value):
    return moved(value, lambda x, y, z, c: (x, y, z, 1 - c))


def swap_chips(value):
    return moved(value, lambda x, y, z, c: (x, y ^ 1, z, c))


def image_to_neighbour(value):
    return moved(value, lambda x, y, z, c: (x, y, z - 1, c) if y % 2 == 0 else (x, y, z + 1, c))


def first_axis(value, by):
    return moved(value, lambda x, y, z, c: (x + by, y, z, c) if c == 0 else (x, y + by, z, c))


def second_axis(value, by):
    return moved(value, lambda x, y, z, c: (x, y + by, z, c) if c == 0 else (x + by, y, z, c))


def along_x(value, by):
    return moved(value, lambda x, y, z, c: (x + by, y, z, c))


def pass_on(value):
    def to(x, y, z, c):
        if c == y // 2:
            return (x, y ^ 2, z, c)
        return (x, y, z, 1 - c)

    return moved(value, to)


def pass_across(value):
    return moved(value, lambda x, y, z, c: (x, y ^ 2, z, 1 - c) if c != y // 2 else None)


def image_down(value):
    return moved(value, lambda x, y, z, c: (x, y, z - 1, c) if y % 2 == 1 and c == 0 else None)


THIRDS = [(n, 384) for n in range(0, D, 384)]


IMAGE_AT = np.array([[0, 1, 4, 5, 100], [2, 3, -2, -1, 6]])
CAPTION_AT = np.array([[0, 1, 2, 3], [2, 3, 0, 1]])
APART = CAPTION_AT[:, None, :] - IMAGE_AT[:, :, None]
TAKEN = ((APART >= -3) & (APART <= 2)).astype(float).tolist()


def nt_dot(a, b):
    return lax.dot_general(a, b, (((1,), (1,)), ((), ())), preferred_element_type=F32)


def fetch(src, dst, sem):
    copy = pltpu.make_async_copy(src, dst, sem)
    copy.start()
    return copy


def by_role(place_ref, choices, sems):
    waits = []
    for k, (zero, one, dst) in enumerate(choices):

        @pl.when(place_ref[0] == 0)
        def _():
            fetch(zero, dst, sems.at[k])

        @pl.when(place_ref[0] == 1)
        def _():
            fetch(one, dst, sems.at[k])

        waits.append(pltpu.make_async_copy(zero, dst, sems.at[k]))
    return waits


def project(feats, head, tmp, rows, squares):
    squares[0:rows] = jnp.zeros((rows, 128), F32)

    @pl.loop(0, 3)
    def _(k):
        at = pl.ds(pl.multiple_of(k * 384, 384), 384)
        p = jnp.dot(feats[0:rows], head[:, at], preferred_element_type=F32)
        tmp[0:rows, at] = p
        p = p * p
        squares[0:rows] += p[:, 0:128] + p[:, 128:256] + p[:, 256:384]

    return lax.rsqrt(jnp.sum(squares[0:rows], axis=1, keepdims=True) + 1e-6)


def one_hot(place_ref, pv):
    core, x, y = place_ref[0], place_ref[2], place_ref[3]

    @pl.loop(0, 3)
    def _(k):
        base = pl.multiple_of(k * 384, 384)
        row = lax.broadcasted_iota(jnp.int32, (384, 1), 0) + base
        group = (row * 7282) >> 16
        one, two = (group >> 5) & 3, (group >> 3) & 3
        to_x = (x + jnp.where(core == 0, one, two)) & 3
        to_y = (y + jnp.where(core == 0, two, one)) & 3
        order = (group & 7) * 144 + row - group * 9 + (to_y & 1) * 72 + (to_y >> 1) * 36 + to_x * 9
        hit = lax.broadcasted_iota(jnp.int32, (384, D), 1) == order
        pv[pl.ds(base, 384)] = jnp.where(hit, 1.0, 0.0).astype(BF16)


def pair_weights(scalars, rows, cols, xs, height, ys, scale_of, gs, label=None):
    sharpness, shift = scalars
    logits = nt_dot(rows, cols) * sharpness + shift
    for i, x in enumerate(xs):
        for j, y in enumerate(ys):
            part = logits[i * height : (i + 1) * height, j * PAD : (j + 1) * PAD]
            scale = scale_of(x, y)
            if label is not None and x == y:
                match = label(x)
                g = jnp.where(match, -scale, scale) * jax.nn.sigmoid(jnp.where(match, -part, part))
            else:
                g = scale * jax.nn.sigmoid(part)
            gs[i * height : (i + 1) * height, j * PAD : (j + 1) * PAD] = g.astype(BF16)


def own_kernel(
    place_ref, sharp_ref, shift_ref, coef_ref, mine_ref, other_ref, im, io, cm, co, wi, wc,
    zx_out, zy_out, ux_out, ix_out, dz_out,
    f, w, tmp, zx, zy, ux, ix, squares, gs, dz, targets, sems,
):
    core = place_ref[0]
    first = by_role(
        place_ref, [(im, co, f.at[0, pl.ds(0, R)]), (io, cm, f.at[0, pl.ds(R, R)]), (wi, wc, w.at[0])],
        sems.at[pl.ds(0, 3)],
    )
    second = by_role(
        place_ref, [(cm, io, f.at[1, pl.ds(0, R)]), (co, im, f.at[1, pl.ds(R, R)]), (wc, wi, w.at[1])],
        sems.at[pl.ds(3, 3)],
    )
    targets[...] = jnp.full((2, PAD), -1, jnp.int32)
    targets[0:1, 0:R] = jnp.where(core == 0, mine_ref[...], other_ref[...])
    targets[1:2, 0:R] = jnp.where(core == 0, other_ref[...], mine_ref[...])
    for wait in first:
        wait.wait()
    inv = project(f.at[0], w.at[0], tmp, 2 * R, ix)
    ix[...] = jnp.broadcast_to(inv, (2 * R, 128))
    unit = tmp[...] * inv
    ux[...] = unit
    zx[...] = unit.astype(BF16)
    outs = [fetch(ux, ux_out, sems.at[6]), fetch(zx, zx_out, sems.at[7]), fetch(ix, ix_out, sems.at[8])]
    for wait in second:
        wait.wait()
    inv = project(f.at[1], w.at[1], tmp, 2 * R, squares)
    for b in range(2):
        zy[b * PAD : b * PAD + R] = (tmp[b * R : (b + 1) * R] * inv[b * R : (b + 1) * R]).astype(BF16)
        zy[b * PAD + R : (b + 1) * PAD] = jnp.zeros((PAD - R, D), BF16)
    outs.append(fetch(zy, zy_out, sems.at[10]))

    def label(k):
        down, across = lax.broadcasted_iota(jnp.int32, (R, PAD), 0), lax.broadcasted_iota(jnp.int32, (R, PAD), 1)
        by_row = jnp.broadcast_to(targets[k : k + 1], (R, PAD))
        by_col = jnp.sum(jnp.where(down == across, by_row, 0), axis=1, keepdims=True)
        target = jnp.where(core == 0, jnp.broadcast_to(by_col, (R, PAD)), by_row)
        return jnp.where(core == 0, across, down) == target

    scalars = (sharp_ref[0], shift_ref[0])
    pair_weights(scalars, zx[...], zy[...], (0, 1), R, (0, 1), lambda x, y: coef_ref[0], gs, label)

    @pl.loop(0, 3)
    def _(k):
        cols = pl.ds(pl.multiple_of(k * 384, 384), 384)
        dz[:, cols] = sharp_ref[0] * jnp.dot(gs[...], zy[:, cols], preferred_element_type=F32)

    outs.append(fetch(dz, dz_out, sems.at[11]))

    for copy in outs:
        copy.wait()


def own_part(place, sharp, shift, coef, mine, other, *operands):
    smem = pl.BlockSpec(memory_space=pltpu.SMEM)
    vmem = pl.BlockSpec(memory_space=pltpu.VMEM)
    hbm = pl.BlockSpec(memory_space=pl.ANY)
    results = [
        ((2 * R, D), BF16), ((2 * PAD, D), BF16), ((2 * R, D), F32), ((2 * R, 128), F32),
        ((2 * R, D), F32),
    ]
    return pl.pallas_call(
        own_kernel,
        out_shape=[jax.ShapeDtypeStruct(*result) for result in results],
        in_specs=[smem] * 4 + [vmem] * 2 + [hbm] * 6,
        out_specs=[hbm] * 5,
        scratch_shapes=[
            pltpu.VMEM((2, 2 * R, D), BF16),
            pltpu.VMEM((2, D, D), BF16),
            pltpu.VMEM((2 * R, D), F32),
            pltpu.VMEM((2 * R, D), BF16),
            pltpu.VMEM((2 * PAD, D), BF16),
            pltpu.VMEM((2 * R, D), F32),
            pltpu.VMEM((2 * R, 128), F32),
            pltpu.VMEM((2 * R, 128), F32),
            pltpu.VMEM((2 * R, 2 * PAD), BF16),
            pltpu.VMEM((2 * R, D), F32),
            pltpu.VMEM((2, PAD), jnp.int32),
            pltpu.SemaphoreType.DMA((13,)),
        ],
        compiler_params=pltpu.CompilerParams(vmem_limit_bytes=60 * 2**20),
        cost_estimate=pl.CostEstimate(flops=6 * 10**9, bytes_accessed=16 * 10**6, transcendentals=500000),
    )(place, sharp, shift, coef, mine, other, *operands)


def turn_kernel(place_ref, im, io, cm, co, pv_out, ft_out, f, pv, ft, sems):
    feats = by_role(
        place_ref, [(im, co, f.at[pl.ds(0, R)]), (io, cm, f.at[pl.ds(R, R)])], sems.at[pl.ds(0, 2)]
    )
    one_hot(place_ref, pv)
    outs = [fetch(pv, pv_out, sems.at[2])]
    for wait in feats:
        wait.wait()

    @pl.loop(0, 3)
    def _(k):
        rows = pl.ds(pl.multiple_of(k * 384, 384), 384)
        ft[rows, 0 : 2 * R] = nt_dot(pv[rows], f[...]).astype(BF16)

    ft[:, 2 * R :] = jnp.zeros((D, 2 * PAD - 2 * R), BF16)
    for copy in outs + [fetch(ft, ft_out, sems.at[3])]:
        copy.wait()


def turn_own(place, *operands):
    hbm = pl.BlockSpec(memory_space=pl.ANY)
    return pl.pallas_call(
        turn_kernel,
        out_shape=[jax.ShapeDtypeStruct((D, D), BF16), jax.ShapeDtypeStruct((D, 2 * PAD), BF16)],
        in_specs=[pl.BlockSpec(memory_space=pltpu.SMEM)] + [hbm] * 4,
        out_specs=[hbm] * 2,
        scratch_shapes=[
            pltpu.VMEM((2 * R, D), BF16),
            pltpu.VMEM((D, D), BF16),
            pltpu.VMEM((D, 2 * PAD), BF16),
            pltpu.SemaphoreType.DMA((4,)),
        ],
        compiler_params=pltpu.CompilerParams(vmem_limit_bytes=60 * 2**20),
        cost_estimate=pl.CostEstimate(flops=2 * 10**9, bytes_accessed=6 * 10**6, transcendentals=0),
    )(place, *operands)


def arrived_kernel(
    place_ref, sharp_ref, shift_ref, coef_ref,
    sm, so, fm, fo, em, eo, wi, wc, order, zx_in, zy_in, ux_in, ix_in, ft_in, dz_in,
    out0, out1, out2, out3,
    fi, fc, w, pv, zx, z, uo, ui, uc, io_, ii, ic, fto, fta, dz, da, gs, dp, sems,
):
    role, y_lo = place_ref[0], place_ref[1]
    scalars = (sharp_ref[0], shift_ref[0])

    def slot(blocks, k):
        return blocks.at[pl.ds(k * PAD, R)]

    images = by_role(place_ref, [(fm, fo, slot(fi, 0)), (fo, fm, slot(fi, 1)), (em, eo, slot(fi, 2))], sems.at[pl.ds(0, 3)])
    images.append(fetch(wi, w.at[0], sems.at[3]))
    for s in range(3):
        fi[s * PAD + R : (s + 1) * PAD] = jnp.zeros((PAD - R, D), BF16)
    for s in range(2):
        fc[s * PAD + R : (s + 1) * PAD] = jnp.zeros((PAD - R, D), BF16)
    dp[2 * R : 2 * PAD] = jnp.zeros((2 * (PAD - R), D), BF16)
    for wait in images:
        wait.wait()
    captions = by_role(place_ref, [(sm, so, slot(fc, 0)), (so, sm, slot(fc, 1))], sems.at[pl.ds(4, 2)])
    captions.append(fetch(wc, w.at[1], sems.at[6]))

    def unit_rows(feats, head, unit, inverse, m, base):
        inv = project(feats, head, unit, m, inverse)
        inverse[...] = jnp.broadcast_to(inv, (m, 128))
        unit[...] = unit[...] * inv
        z[pl.ds(pl.multiple_of(base, PAD), m)] = unit[...].astype(BF16)

    unit_rows(fi, w.at[0], ui, ii, 3 * PAD, role * 5 * PAD)
    for wait in captions:
        wait.wait()
    order_copy = fetch(order, pv, sems.at[7])
    late = [
        fetch(zx_in, zx, sems.at[8]),
        fetch(zy_in, z.at[pl.ds(3 * PAD, 2 * PAD)], sems.at[9]),
        fetch(ux_in, uo, sems.at[10]),
        fetch(ix_in, io_, sems.at[11]),
        fetch(dz_in, dz, sems.at[12]),
        fetch(ft_in, fto, sems.at[13]),
    ]
    unit_rows(fc, w.at[1], uc, ic, 2 * PAD, (1 - role) * 5 * PAD)
    order_copy.wait()

    def turn(feats, m):
        @pl.loop(0, 3)
        def _(k):
            rows = pl.ds(pl.multiple_of(k * 384, 384), 384)
            fta[rows, 0:m] = nt_dot(pv[rows], feats[...]).astype(BF16)

    @pl.when(role == 0)
    def _():
        turn(fi, 3 * PAD)

    @pl.when(role == 1)
    def _():
        turn(fc, 2 * PAD)
        fta[:, 2 * PAD : 3 * PAD] = jnp.zeros((D, PAD), BF16)

    for copy in late:
        copy.wait()

    def spread(m, cols, y0, y1, kept, unit, inverse, base):
        @pl.loop(0, 3)
        def _(k):
            at = pl.ds(pl.multiple_of(k * 384, 384), 384)
            d = scalars[0] * jnp.dot(gs[0:m, 0:cols], z[y0 * PAD : y1 * PAD, at], preferred_element_type=F32)
            if kept:
                d = d + dz[:, at]
            da[0:m, at] = d

        along = jnp.sum(da[0:m] * unit[0:m], axis=1, keepdims=True)
        dp[base : base + m] = ((da[0:m] - unit[0:m] * along) * inverse[0:m, 0:1]).astype(BF16)

    def scale(image, caption):
        return coef_ref[0] * jnp.where(y_lo == 0, TAKEN[0][image][caption], TAKEN[1][image][caption])

    def by_image(x, y):
        return scale(x, y)

    def by_caption(x, y):
        return scale(y, x)

    @pl.when(role == 0)
    def _():
        pair_weights(scalars, zx[...], z[5 * PAD : 7 * PAD], (0, 1), R, (2, 3), by_image, gs)
        spread(2 * R, 2 * PAD, 5, 7, True, uo, io_, 0)
        pair_weights(scalars, z[0 : 2 * PAD], z[4 * PAD : 7 * PAD], (2, 3), PAD, (1, 2, 3), by_image, gs)
        spread(2 * PAD, 3 * PAD, 4, 7, False, ui, ii, 2 * PAD)
        pair_weights(scalars, z[2 * PAD : 3 * PAD], z[4 * PAD : 5 * PAD], (4,), PAD, (1,), by_image, gs)
        spread(PAD, PAD, 4, 5, False, ui.at[2 * PAD : 3 * PAD], ii.at[2 * PAD : 3 * PAD], 4 * PAD)

    @pl.when(role == 1)
    def _():
        pair_weights(scalars, zx[...], z[5 * PAD : 8 * PAD], (0, 1), R, (2, 3, 4), by_caption, gs)
        spread(2 * R, 3 * PAD, 5, 8, True, uo, io_, 0)
        pair_weights(scalars, z[0 : 2 * PAD], z[3 * PAD : 7 * PAD], (2, 3), PAD, (0, 1, 2, 3), by_caption, gs)
        spread(2 * PAD, 4 * PAD, 3, 7, False, uc, ic, 2 * PAD)
        dp[4 * PAD : 5 * PAD] = jnp.zeros((PAD, D), BF16)

    @pl.loop(0, 3)
    def _(k):
        at = pl.ds(pl.multiple_of(k * 384, 384), 384)
        own = dp[0 : 2 * PAD, at]
        rest = dp[2 * PAD : 5 * PAD, at]
        for i, out in enumerate((out0, out1, out2, out3)):
            rows = slice(i * 288, (i + 1) * 288)
            out[:, at] = (
                jnp.dot(fto[rows], own, preferred_element_type=F32)
                + jnp.dot(fta[rows], rest, preferred_element_type=F32)
            ).astype(BF16)


def arrived_part(place, sharp, shift, coef, *operands):
    smem = pl.BlockSpec(memory_space=pltpu.SMEM)
    vmem = pl.BlockSpec(memory_space=pltpu.VMEM)
    return pl.pallas_call(
        arrived_kernel,
        out_shape=[jax.ShapeDtypeStruct((D // 4, D), BF16)] * 4,
        in_specs=[smem] * 4 + [pl.BlockSpec(memory_space=pl.ANY)] * 15,
        out_specs=[vmem] * 4,
        scratch_shapes=[
            pltpu.VMEM((3 * PAD, D), BF16),
            pltpu.VMEM((2 * PAD, D), BF16),
            pltpu.VMEM((2, D, D), BF16),
            pltpu.VMEM((D, D), BF16),
            pltpu.VMEM((2 * R, D), BF16),
            pltpu.VMEM((8 * PAD, D), BF16),
            pltpu.VMEM((2 * R, D), F32),
            pltpu.VMEM((3 * PAD, D), F32),
            pltpu.VMEM((2 * PAD, D), F32),
            pltpu.VMEM((2 * R, 128), F32),
            pltpu.VMEM((3 * PAD, 128), F32),
            pltpu.VMEM((2 * PAD, 128), F32),
            pltpu.VMEM((D, 2 * PAD), BF16),
            pltpu.VMEM((D, 3 * PAD), BF16),
            pltpu.VMEM((2 * R, D), F32),
            pltpu.VMEM((3 * PAD, D), F32),
            pltpu.VMEM((3 * PAD, 4 * PAD), BF16),
            pltpu.VMEM((5 * PAD, D), BF16),
            pltpu.SemaphoreType.DMA((14,)),
        ],
        compiler_params=pltpu.CompilerParams(vmem_limit_bytes=60 * 2**20),
        cost_estimate=pl.CostEstimate(flops=14 * 10**9, bytes_accessed=20 * 10**6, transcendentals=800000),
    )(place, sharp, shift, coef, *operands)


def join_kernel(place_ref, one, two, three, four, image_out, caption_out, held):
    for k, piece in enumerate((one, two, three, four)):
        held[k] = piece[...]
    for place in range(NX):
        back = (place_ref[2] - place) & 3
        for head, out in enumerate((image_out, caption_out)):
            for row in range(9):
                at = place * 9 + row
                for n in range(9):
                    out[at : at + 1, n * 128 : (n + 1) * 128] = held[back, head, row * 9 + n : row * 9 + n + 1]


def join_rows(place, *pieces):
    vmem = pl.BlockSpec(memory_space=pltpu.VMEM)
    return pl.pallas_call(
        join_kernel,
        out_shape=[jax.ShapeDtypeStruct((36, D), F32)] * 2,
        in_specs=[pl.BlockSpec(memory_space=pltpu.SMEM)] + [vmem] * 4,
        out_specs=[vmem] * 2,
        scratch_shapes=[pltpu.VMEM((4, 2, 81, 128), F32)],
    )(place, *pieces)


def local(
    picture_encoder_features,
    text_encoder_features,
    picture_projector,
    text_projector,
    matching_target,
    sharpness_param,
    offset_shift,
    objective_multiplier,
):
    place = lax.axis_index("dp")
    core, y_lo = place % 2, (place // 2) % 2
    x, y_hi = lax.axis_index("replica") // 2, lax.axis_index("replica") % 2
    y = y_hi * 2 + y_lo
    role = jnp.stack([core, y_lo, x, y]).astype(jnp.int32)
    coefficient = objective_multiplier / (lax.axis_size("dp") * R)

    own_img = swap_cores(picture_encoder_features)
    own_cap = swap_cores(text_encoder_features)
    target_other = swap_cores(matching_target)
    cap, img, target_other = lax.optimization_barrier(
        (text_encoder_features, picture_encoder_features, target_other)
    )
    cap_sib = swap_chips(cap)
    img_far = image_to_neighbour(img)
    img_extra = image_down(img)

    blocks = (picture_encoder_features, own_img, text_encoder_features, own_cap)
    *kept, from_own = own_part(
        role, sharpness_param, offset_shift, coefficient, matching_target[None], target_other[None],
        *blocks, picture_projector, text_projector,
    )
    cap_sib, img_far, img_extra, kept, from_own, blocks = lax.optimization_barrier(
        (cap_sib, img_far, img_extra, kept, from_own, blocks)
    )
    cap_sib_other = swap_cores(cap_sib)
    img_far_other = swap_cores(img_far)
    img_extra_other = swap_cores(img_extra)
    order, turned = turn_own(role, *blocks)
    parts = arrived_part(
        role, sharpness_param, offset_shift, coefficient,
        cap_sib, cap_sib_other, img_far, img_far_other, img_extra, img_extra_other,
        picture_projector, text_projector, order, *kept, turned, from_own,
    )

    one = [parts[0]] + [first_axis(parts[by], by) for by in (1, 3, 2)]
    one = sum(v.astype(F32) for v in one).astype(BF16)
    pieces = [one[by * 72 : (by + 1) * 72] for by in range(4)]
    two = [pieces[0]] + [second_axis(pieces[by], by) for by in (1, 3, 2)]
    two = sum(v.astype(F32) for v in two).astype(BF16).reshape(NZ, 81, 128)
    three = lax.all_to_all(two, AXES, 0, 0, axis_index_groups=ALONG_Z)
    mine = jnp.sum(three.astype(F32), axis=0)

    first = core == 0
    ring, cross = pass_on(mine), pass_across(mine)
    home = core == y_hi
    image_piece = jnp.where(home & first, mine, jnp.where(home | first, ring, cross))
    caption_piece = jnp.where(home & first, ring, jnp.where(home, mine, jnp.where(first, cross, ring)))
    both = jnp.stack([image_piece, caption_piece])
    return join_rows(role, both, *[along_x(both, by) for by in (1, 2, 3)])


def solution(mesh):
    placed = (
        P(("dp", "replica"), None),
        P(("dp", "replica"), None),
        P(),
        P(),
        P(("dp", "replica")),
        P(),
        P(),
        P(),
    )
    return jax.shard_map(
        local, mesh=mesh, in_specs=placed, out_specs=(P("dp", None), P("dp", None)), check_vma=False
    )
```

profile of v0, /device:TPU:1, one launch (start us, length us, event | category | flops | bytes accessed | tf_op | source)
XLA Modules:
  0.0 125.6 jit_solution(5877028967481722130)
XLA Ops:
  0.6 3.3 %collective-permute-start.4 = (bf16[224,1152]{1,0:T(8,128)(2,1)}, bf16[224,1152]{1,0:T(8,128)(2,1)S(1)}, u32[]{:S(2)}, u32[]{:S(2)}) collective-permute-start(bf16[224,1152]{1,0:T(8,128)(2,1)} %im.2), channel_id=1, source_target_pairs={{0,8},{8,0},{32,40},{40,32},{64,72},{72,64},{96,104},{104,96},{128... | collective-permute-start | bytes 1548296 | tf_op jit(solution)/shard_map/ppermute | solution.py:32
  4.5 0.6 pad_add_fusion.place_ref
  7.1 3.9 %collective-permute-start.2 = (bf16[224,1152]{1,0:T(8,128)(2,1)}, bf16[224,1152]{1,0:T(8,128)(2,1)S(1)}, u32[]{:S(2)}, u32[]{:S(2)}) collective-permute-start(bf16[224,1152]{1,0:T(8,128)(2,1)} %im.2), channel_id=1, source_target_pairs={{0,224},{8,232},{32,0},{40,8},{64,32},{72,40},{96,64},{104,72},{12... | collective-permute-start | bytes 1548296 | tf_op jit(solution)/shard_map/ppermute | solution.py:32
  11.0 0.7 collective-permute-start.3
  11.8 0.8 copy-done.4
  12.8 11.3 %shard_map.95 = (bf16[448,1152]{1,0:T(8,128)(2,1)}, bf16[512,1152]{1,0:T(8,128)(2,1)}, f32[448,1152]{1,0:T(8,128)}, f32[448,128]{1,0:T(8,128)}, f32[448,1152]{1,0:T(8,128)}) custom-call(s32[4]{0:T(128)} %pad_add_fusion.place_ref, f32[1]{0:T(128)S(6)} %copy.10.sharp_ref, f32[1]{0:T(128)S(6)} %copy.11.shift_ref, f32[1]{0:T(128)S(6)} %div.24.coef_ref, ...), custom_call_target="tpu_custom_call" | custom-call | flops 6000000000 | bytes 16000000 | tf_op jit(solution)/shard_map/pallas_call | solution.py:218
  24.2 3.2 %collective-permute-start.6 = (bf16[224,1152]{1,0:T(8,128)(2,1)S(1)}, bf16[224,1152]{1,0:T(8,128)(2,1)S(1)}, u32[]{:S(2)}, u32[]{:S(2)}) collective-permute-start(bf16[224,1152]{1,0:T(8,128)(2,1)S(1)} %collective-permute-done.1.sm), channel_id=1, source_target_pairs={{0,8},{8,0},{32,40},{40,32},{64,72},{72,64},{96,104},{104,96},{128... | collective-permute-start | bytes 1548296 | tf_op jit(solution)/shard_map/ppermute | solution.py:32
  27.9 5.1 %shard_map.96 = (bf16[1152,1152]{1,0:T(8,128)(2,1)}, bf16[1152,512]{1,0:T(8,128)(2,1)}) custom-call(s32[4]{0:T(128)} %pad_add_fusion.place_ref, bf16[224,1152]{1,0:T(8,128)(2,1)} %im.2, bf16[224,1152]{1,0:T(8,128)(2,1)} %copy-done.4, bf16[224,1152]{1,0:T(8,128)(2,1)} %cm.2, bf16[224,1152]{1,0:T(8,128)(2,1)} %copy-done.5), custom_call_target="tpu_custom_call" | custom-call | flops 2000000000 | bytes 6000000 | tf_op jit(solution)/shard_map/pallas_call | solution.py:263
  33.1 0.7 copy-done.9
  34.2 25.3 %shard_map.97 = (bf16[288,1152]{1,0:T(8,128)(2,1)}, bf16[288,1152]{1,0:T(8,128)(2,1)}, bf16[288,1152]{1,0:T(8,128)(2,1)}, bf16[288,1152]{1,0:T(8,128)(2,1)}) custom-call(s32[4]{0:T(128)} %pad_add_fusion.place_ref, f32[1]{0:T(128)S(6)} %copy.10.sharp_ref, f32[1]{0:T(128)S(6)} %copy.11.shift_ref, f32[1]{0:T(128)S(6)} %div.24.coef_ref, ...), custom_call_target="tpu_custom_call" | custom-call | flops 14000000000 | bytes 20000000 | tf_op jit(solution)/shard_map/pallas_call | solution.py:396
  59.5 1.3 %collective-permute-start.10 = (bf16[288,1152]{1,0:T(8,128)(2,1)}, bf16[288,1152]{1,0:T(8,128)(2,1)S(1)}, u32[]{:S(2)}, u32[]{:S(2)}) collective-permute-start(bf16[288,1152]{1,0:T(8,128)(2,1)} %get-tuple-element.52), channel_id=1, source_target_pairs={{0,6},{8,25},{32,38},{40,57},{64,70},{72,89},{96,102},{104,121},{1... | collective-permute-start | bytes 1990664 | tf_op jit(solution)/shard_map/ppermute | solution.py:32
  60.8 1.5 %collective-permute-start.11 = (bf16[288,1152]{1,0:T(8,128)(2,1)}, bf16[288,1152]{1,0:T(8,128)(2,1)S(1)}, u32[]{:S(2)}, u32[]{:S(2)}) collective-permute-start(bf16[288,1152]{1,0:T(8,128)(2,1)} %get-tuple-element.53), channel_id=1, source_target_pairs={{0,4},{8,9},{32,36},{40,41},{64,68},{72,73},{96,100},{104,105},{12... | collective-permute-start | bytes 1990664 | tf_op jit(solution)/shard_map/ppermute | solution.py:32
  62.3 0.8 collective-permute-start.9
  63.1 6.5 %collective-permute-done.10 = bf16[288,1152]{1,0:T(8,128)(2,1)S(1)} collective-permute-done((bf16[288,1152]{1,0:T(8,128)(2,1)}, bf16[288,1152]{1,0:T(8,128)(2,1)S(1)}, u32[]{:S(2)}, u32[]{:S(2)}) %collective-permute-start.10) | collective-permute-done | bytes 663584 | tf_op jit(solution)/shard_map/ppermute | solution.py:32
  69.6 2.7 %collective-permute-done.11 = bf16[288,1152]{1,0:T(8,128)(2,1)S(1)} collective-permute-done((bf16[288,1152]{1,0:T(8,128)(2,1)}, bf16[288,1152]{1,0:T(8,128)(2,1)S(1)}, u32[]{:S(2)}, u32[]{:S(2)}) %collective-permute-start.11) | collective-permute-done | bytes 663584 | tf_op jit(solution)/shard_map/ppermute | solution.py:32
  72.4 7.1 %collective-permute-done.9 = bf16[288,1152]{1,0:T(8,128)(2,1)S(1)} collective-permute-done((bf16[288,1152]{1,0:T(8,128)(2,1)}, bf16[288,1152]{1,0:T(8,128)(2,1)S(1)}, u32[]{:S(2)}, u32[]{:S(2)}) %collective-permute-start.9) | collective-permute-done | bytes 663584 | tf_op jit(solution)/shard_map/ppermute | solution.py:32
  79.4 1.4 %add_convert_fusion = bf16[288,1152]{1,0:T(8,128)(2,1)S(1)} fusion(bf16[288,1152]{1,0:T(8,128)(2,1)S(1)} %collective-permute-done.11, bf16[288,1152]{1,0:T(8,128)(2,1)S(1)} %collective-permute-done.10, bf16[288,1152]{1,0:T(8,128)(2,1)S(1)} %collective-permute-done.9, bf16[288,1152]{1,0:T(8,128)(2,1)} %get-tuple-element.50), kind=kLoop, calls=%fused_computation | loop fusion | flops 2654208 | bytes 3317760 | tf_op jit(solution)/shard_map/convert_element_type | solution.py:496
  80.9 1.0 collective-permute-start.12
  81.9 1.8 %collective-permute-start.13 = (bf16[72,1152]{1,0:T(8,128)(2,1)S(1)}, bf16[72,1152]{1,0:T(8,128)(2,1)S(1)}, u32[]{:S(2)}, u32[]{:S(2)}) collective-permute-start(bf16[72,1152]{1,0:T(8,128)(2,1)S(1)} %get-tuple-element.56), channel_id=1, source_target_pairs={{0,17},{8,14},{32,49},{40,46},{64,81},{72,78},{96,113},{104,110},{... | collective-permute-start | bytes 497672 | tf_op jit(solution)/shard_map/ppermute | solution.py:32
  83.7 1.2 collective-permute-start.14
  84.9 1.5 %collective-permute-done.12 = bf16[72,1152]{1,0:T(8,128)(2,1)S(1)} collective-permute-done((bf16[72,1152]{1,0:T(8,128)(2,1)S(1)}, bf16[72,1152]{1,0:T(8,128)(2,1)S(1)}, u32[]{:S(2)}, u32[]{:S(2)}) %collective-permute-start.12) | collective-permute-done | bytes 165920 | tf_op jit(solution)/shard_map/ppermute | solution.py:32
  86.4 1.3 %collective-permute-done.13 = bf16[72,1152]{1,0:T(8,128)(2,1)S(1)} collective-permute-done((bf16[72,1152]{1,0:T(8,128)(2,1)S(1)}, bf16[72,1152]{1,0:T(8,128)(2,1)S(1)}, u32[]{:S(2)}, u32[]{:S(2)}) %collective-permute-start.13) | collective-permute-done | bytes 165920 | tf_op jit(solution)/shard_map/ppermute | solution.py:32
  87.7 1.6 %collective-permute-done.14 = bf16[72,1152]{1,0:T(8,128)(2,1)S(1)} collective-permute-done((bf16[72,1152]{1,0:T(8,128)(2,1)S(1)}, bf16[72,1152]{1,0:T(8,128)(2,1)S(1)}, u32[]{:S(2)}, u32[]{:S(2)}) %collective-permute-start.14) | collective-permute-done | bytes 165920 | tf_op jit(solution)/shard_map/ppermute | solution.py:32
  89.7 13.8 %all_to_all.5 = bf16[8,81,128]{2,1,0:T(8,128)(2,1)S(1)} all-to-all(bf16[8,81,128]{2,1,0:T(8,128)(2,1)S(1)} %reshape.7), channel_id=1, replica_groups={{0,32,64,96,128,160,192,224},{8,40,72,104,136,168,200,232},{16,48,80,11..., dimensions={0} | all-to-all | bytes 331776 | tf_op jit(solution)/shard_map/all_to_all | solution.py:500
  103.5 6.2 %collective-permute-start.15 = (f32[81,128]{1,0:T(8,128)S(1)}, f32[81,128]{1,0:T(8,128)S(1)}, u32[]{:S(2)}, u32[]{:S(2)}) collective-permute-start(f32[81,128]{1,0:T(8,128)S(1)} %convert_reduce_fusion), channel_id=1, source_target_pairs={{0,1},{8,0},{32,33},{40,32},{64,65},{72,64},{96,97},{104,96},{128,... | collective-permute-start | bytes 124424 | tf_op jit(solution)/shard_map/ppermute | solution.py:32
  109.8 3.2 %collective-permute-start.16 = (f32[81,128]{1,0:T(8,128)S(1)}, f32[81,128]{1,0:T(8,128)S(1)}, u32[]{:S(2)}, u32[]{:S(2)}) collective-permute-start(f32[81,128]{1,0:T(8,128)S(1)} %convert_reduce_fusion), channel_id=1, source_target_pairs={{8,1},{40,33},{72,65},{104,97},{136,129},{168,161},{200,193},{232,... | collective-permute-start | bytes 124424 | tf_op jit(solution)/shard_map/ppermute | solution.py:32
  113.0 3.6 %collective-permute-done.16 = f32[81,128]{1,0:T(8,128)S(1)} collective-permute-done((f32[81,128]{1,0:T(8,128)S(1)}, f32[81,128]{1,0:T(8,128)S(1)}, u32[]{:S(2)}, u32[]{:S(2)}) %collective-permute-start.16) | collective-permute-done | bytes 41504 | tf_op jit(solution)/shard_map/ppermute | solution.py:32
  116.7 1.5 %collective-permute-start.18 = (f32[2,81,128]{2,1,0:T(8,128)S(1)}, f32[2,81,128]{2,1,0:T(8,128)S(1)}, u32[]{:S(2)}, u32[]{:S(2)}) collective-permute-start(f32[2,81,128]{2,1,0:T(8,128)S(1)} %pad_maximum_fusion.one), channel_id=1, source_target_pairs={{0,4},{8,12},{32,36},{40,44},{64,68},{72,76},{96,100},{104,108},{1... | collective-permute-start | bytes 248840 | tf_op jit(solution)/shard_map/ppermute | solution.py:32
  118.2 1.2 collective-permute-start.19
  119.4 2.9 %collective-permute-done.17.two = f32[2,81,128]{2,1,0:T(8,128)S(1)} collective-permute-done((f32[2,81,128]{2,1,0:T(8,128)S(1)}, f32[2,81,128]{2,1,0:T(8,128)S(1)}, u32[]{:S(2)}, u32[]{:S(2)}) %collective-permute-start.17) | collective-permute-done | bytes 82976 | tf_op jit(solution)/shard_map/ppermute | solution.py:32
  123.0 0.6 copy-done.3
  123.6 2.0 %shard_map.98 = (f32[36,1152]{1,0:T(8,128)}, f32[36,1152]{1,0:T(8,128)}) custom-call(s32[4]{0:T(128)} %pad_add_fusion.place_ref, f32[2,81,128]{2,1,0:T(8,128)} %copy-done, f32[2,81,128]{2,1,0:T(8,128)} %copy-done.1, f32[2,81,128]{2,1,0:T(8,128)} %copy-done.2, f32[2,81,128]{2,1,0:T(8,128)} %copy-done.3), custom_call_target="tpu_custom_call" | custom-call | tf_op jit(solution)/shard_map/pallas_call | solution.py:441
  (47 shorter events, 2.9 us)
Async XLA Ops:
  0.6 11.2 %collective-permute-start.4 = (bf16[224,1152]{1,0:T(8,128)(2,1)}, bf16[224,1152]{1,0:T(8,128)(2,1)S(1)}, u32[]{:S(2)}, u32[]{:S(2)}) collective-permute-start(bf16[224,1152]{1,0:T(8,128)(2,1)} %im.2), channel_id=1, source_target_pairs={{0,8},{8,0},{32,40},{40,32},{64,72},{72,64},{96,104},{104,96},{128... | collective-permute-start | bytes 1548296 | tf_op jit(solution)/shard_map/ppermute | solution.py:32
  4.0 7.8 %collective-permute-start.5 = (bf16[224,1152]{1,0:T(8,128)(2,1)}, bf16[224,1152]{1,0:T(8,128)(2,1)S(1)}, u32[]{:S(2)}, u32[]{:S(2)}) collective-permute-start(bf16[224,1152]{1,0:T(8,128)(2,1)} %cm.2), channel_id=1, source_target_pairs={{0,8},{8,0},{32,40},{40,32},{64,72},{72,64},{96,104},{104,96},{128... | collective-permute-start | bytes 1548296 | tf_op jit(solution)/shard_map/ppermute | solution.py:32
  4.1 3.0 %collective-permute-start = (s32[224]{0:T(256)}, s32[224]{0:T(256)S(1)}, u32[]{:S(2)}, u32[]{:S(2)}) collective-permute-start(s32[224]{0:T(256)} %param.12), channel_id=1, source_target_pairs={{0,8},{8,0},{32,40},{40,32},{64,72},{72,64},{96,104},{104,96},{128... | collective-permute-start | bytes 2696 | tf_op jit(solution)/shard_map/ppermute | solution.py:32
  7.0 4.8 %copy-start.12 = (s32[224]{0:T(256)}, s32[224]{0:T(256)S(1)}, u32[]{:S(2)}) copy-start(s32[224]{0:T(256)S(1)} %collective-permute-done) | copy-start | bytes 2692
  7.1 17.1 %collective-permute-start.2 = (bf16[224,1152]{1,0:T(8,128)(2,1)}, bf16[224,1152]{1,0:T(8,128)(2,1)S(1)}, u32[]{:S(2)}, u32[]{:S(2)}) collective-permute-start(bf16[224,1152]{1,0:T(8,128)(2,1)} %im.2), channel_id=1, source_target_pairs={{0,224},{8,232},{32,0},{40,8},{64,32},{72,40},{96,64},{104,72},{12... | collective-permute-start | bytes 1548296 | tf_op jit(solution)/shard_map/ppermute | solution.py:32
  11.0 13.2 %collective-permute-start.3 = (bf16[224,1152]{1,0:T(8,128)(2,1)}, bf16[224,1152]{1,0:T(8,128)(2,1)S(1)}, u32[]{:S(2)}, u32[]{:S(2)}) collective-permute-start(bf16[224,1152]{1,0:T(8,128)(2,1)} %im.2), channel_id=1, source_target_pairs={{16,240},{48,16},{80,48},{112,80},{144,112},{176,144},{208,176},{2... | collective-permute-start | bytes 1548296 | tf_op jit(solution)/shard_map/ppermute | solution.py:32
  11.7 12.5 %collective-permute-start.1 = (bf16[224,1152]{1,0:T(8,128)(2,1)}, bf16[224,1152]{1,0:T(8,128)(2,1)S(1)}, u32[]{:S(2)}, u32[]{:S(2)}) collective-permute-start(bf16[224,1152]{1,0:T(8,128)(2,1)} %cm.2), channel_id=1, source_target_pairs={{0,16},{8,24},{32,48},{40,56},{64,80},{72,88},{96,112},{104,120},{... | collective-permute-start | bytes 1548296 | tf_op jit(solution)/shard_map/ppermute | solution.py:32
  11.8 0.8 copy-start.4
  11.8 1.0 copy-start.5
  24.1 8.9 %copy-start.6 = (bf16[224,1152]{1,0:T(8,128)(2,1)}, bf16[224,1152]{1,0:T(8,128)(2,1)S(1)}, u32[]{:S(2)}) copy-start(bf16[224,1152]{1,0:T(8,128)(2,1)S(1)} %collective-permute-done.2.fm) | copy-start | bytes 1548292
  24.2 8.9 %copy-start.7 = (bf16[224,1152]{1,0:T(8,128)(2,1)}, bf16[224,1152]{1,0:T(8,128)(2,1)S(1)}, u32[]{:S(2)}) copy-start(bf16[224,1152]{1,0:T(8,128)(2,1)S(1)} %collective-permute-done.3.em) | copy-start | bytes 1548292
  24.2 8.9 %copy-start.8 = (bf16[224,1152]{1,0:T(8,128)(2,1)}, bf16[224,1152]{1,0:T(8,128)(2,1)S(1)}, u32[]{:S(2)}) copy-start(bf16[224,1152]{1,0:T(8,128)(2,1)S(1)} %collective-permute-done.1.sm) | copy-start | bytes 1548292
  24.2 8.9 %collective-permute-start.6 = (bf16[224,1152]{1,0:T(8,128)(2,1)S(1)}, bf16[224,1152]{1,0:T(8,128)(2,1)S(1)}, u32[]{:S(2)}, u32[]{:S(2)}) collective-permute-start(bf16[224,1152]{1,0:T(8,128)(2,1)S(1)} %collective-permute-done.1.sm), channel_id=1, source_target_pairs={{0,8},{8,0},{32,40},{40,32},{64,72},{72,64},{96,104},{104,96},{128... | collective-permute-start | bytes 1548296 | tf_op jit(solution)/shard_map/ppermute | solution.py:32
  27.4 5.6 %collective-permute-start.7 = (bf16[224,1152]{1,0:T(8,128)(2,1)S(1)}, bf16[224,1152]{1,0:T(8,128)(2,1)S(1)}, u32[]{:S(2)}, u32[]{:S(2)}) collective-permute-start(bf16[224,1152]{1,0:T(8,128)(2,1)S(1)} %collective-permute-done.2.fm), channel_id=1, source_target_pairs={{0,8},{8,0},{32,40},{40,32},{64,72},{72,64},{96,104},{104,96},{128... | collective-permute-start | bytes 1548296 | tf_op jit(solution)/shard_map/ppermute | solution.py:32
  27.5 5.6 %collective-permute-start.8 = (bf16[224,1152]{1,0:T(8,128)(2,1)S(1)}, bf16[224,1152]{1,0:T(8,128)(2,1)S(1)}, u32[]{:S(2)}, u32[]{:S(2)}) collective-permute-start(bf16[224,1152]{1,0:T(8,128)(2,1)S(1)} %collective-permute-done.3.em), channel_id=1, source_target_pairs={{0,8},{8,0},{32,40},{40,32},{64,72},{72,64},{96,104},{104,96},{128... | collective-permute-start | bytes 1548296 | tf_op jit(solution)/shard_map/ppermute | solution.py:32
  33.1 0.8 copy-start.9
  33.1 1.0 copy-start.10
  33.1 1.1 copy-start.11
  59.5 10.1 %collective-permute-start.10 = (bf16[288,1152]{1,0:T(8,128)(2,1)}, bf16[288,1152]{1,0:T(8,128)(2,1)S(1)}, u32[]{:S(2)}, u32[]{:S(2)}) collective-permute-start(bf16[288,1152]{1,0:T(8,128)(2,1)} %get-tuple-element.52), channel_id=1, source_target_pairs={{0,6},{8,25},{32,38},{40,57},{64,70},{72,89},{96,102},{104,121},{1... | collective-permute-start | bytes 1990664 | tf_op jit(solution)/shard_map/ppermute | solution.py:32
  60.8 11.6 %collective-permute-start.11 = (bf16[288,1152]{1,0:T(8,128)(2,1)}, bf16[288,1152]{1,0:T(8,128)(2,1)S(1)}, u32[]{:S(2)}, u32[]{:S(2)}) collective-permute-start(bf16[288,1152]{1,0:T(8,128)(2,1)} %get-tuple-element.53), channel_id=1, source_target_pairs={{0,4},{8,9},{32,36},{40,41},{64,68},{72,73},{96,100},{104,105},{12... | collective-permute-start | bytes 1990664 | tf_op jit(solution)/shard_map/ppermute | solution.py:32
  62.3 17.1 %collective-permute-start.9 = (bf16[288,1152]{1,0:T(8,128)(2,1)}, bf16[288,1152]{1,0:T(8,128)(2,1)S(1)}, u32[]{:S(2)}, u32[]{:S(2)}) collective-permute-start(bf16[288,1152]{1,0:T(8,128)(2,1)} %get-tuple-element.51), channel_id=1, source_target_pairs={{0,2},{8,24},{32,34},{40,56},{64,66},{72,88},{96,98},{104,120},{12... | collective-permute-start | bytes 1990664 | tf_op jit(solution)/shard_map/ppermute | solution.py:32
  80.9 5.5 %collective-permute-start.12 = (bf16[72,1152]{1,0:T(8,128)(2,1)S(1)}, bf16[72,1152]{1,0:T(8,128)(2,1)S(1)}, u32[]{:S(2)}, u32[]{:S(2)}) collective-permute-start(bf16[72,1152]{1,0:T(8,128)(2,1)S(1)} %get-tuple-element.54), channel_id=1, source_target_pairs={{0,16},{8,10},{32,48},{40,42},{64,80},{72,74},{96,112},{104,106},{... | collective-permute-start | bytes 497672 | tf_op jit(solution)/shard_map/ppermute | solution.py:32
  81.9 5.8 %collective-permute-start.13 = (bf16[72,1152]{1,0:T(8,128)(2,1)S(1)}, bf16[72,1152]{1,0:T(8,128)(2,1)S(1)}, u32[]{:S(2)}, u32[]{:S(2)}) collective-permute-start(bf16[72,1152]{1,0:T(8,128)(2,1)S(1)} %get-tuple-element.56), channel_id=1, source_target_pairs={{0,17},{8,14},{32,49},{40,46},{64,81},{72,78},{96,113},{104,110},{... | collective-permute-start | bytes 497672 | tf_op jit(solution)/shard_map/ppermute | solution.py:32
  83.7 5.7 %collective-permute-start.14 = (bf16[72,1152]{1,0:T(8,128)(2,1)S(1)}, bf16[72,1152]{1,0:T(8,128)(2,1)S(1)}, u32[]{:S(2)}, u32[]{:S(2)}) collective-permute-start(bf16[72,1152]{1,0:T(8,128)(2,1)S(1)} %get-tuple-element.55), channel_id=1, source_target_pairs={{0,1},{8,12},{32,33},{40,44},{64,65},{72,76},{96,97},{104,108},{12... | collective-permute-start | bytes 497672 | tf_op jit(solution)/shard_map/ppermute | solution.py:32
  103.5 9.5 %collective-permute-start.15 = (f32[81,128]{1,0:T(8,128)S(1)}, f32[81,128]{1,0:T(8,128)S(1)}, u32[]{:S(2)}, u32[]{:S(2)}) collective-permute-start(f32[81,128]{1,0:T(8,128)S(1)} %convert_reduce_fusion), channel_id=1, source_target_pairs={{0,1},{8,0},{32,33},{40,32},{64,65},{72,64},{96,97},{104,96},{128,... | collective-permute-start | bytes 124424 | tf_op jit(solution)/shard_map/ppermute | solution.py:32
  109.8 6.9 %collective-permute-start.16 = (f32[81,128]{1,0:T(8,128)S(1)}, f32[81,128]{1,0:T(8,128)S(1)}, u32[]{:S(2)}, u32[]{:S(2)}) collective-permute-start(f32[81,128]{1,0:T(8,128)S(1)} %convert_reduce_fusion), channel_id=1, source_target_pairs={{8,1},{40,33},{72,65},{104,97},{136,129},{168,161},{200,193},{232,... | collective-permute-start | bytes 124424 | tf_op jit(solution)/shard_map/ppermute | solution.py:32
  116.6 6.2 %copy-start = (f32[2,81,128]{2,1,0:T(8,128)}, f32[2,81,128]{2,1,0:T(8,128)S(1)}, u32[]{:S(2)}) copy-start(f32[2,81,128]{2,1,0:T(8,128)S(1)} %pad_maximum_fusion.one) | copy-start | bytes 248836
  116.7 5.6 %collective-permute-start.17 = (f32[2,81,128]{2,1,0:T(8,128)S(1)}, f32[2,81,128]{2,1,0:T(8,128)S(1)}, u32[]{:S(2)}, u32[]{:S(2)}) collective-permute-start(f32[2,81,128]{2,1,0:T(8,128)S(1)} %pad_maximum_fusion.one), channel_id=1, source_target_pairs={{0,2},{8,10},{32,34},{40,42},{64,66},{72,74},{96,98},{104,106},{12... | collective-permute-start | bytes 248840 | tf_op jit(solution)/shard_map/ppermute | solution.py:32
  116.7 5.5 %collective-permute-start.18 = (f32[2,81,128]{2,1,0:T(8,128)S(1)}, f32[2,81,128]{2,1,0:T(8,128)S(1)}, u32[]{:S(2)}, u32[]{:S(2)}) collective-permute-start(f32[2,81,128]{2,1,0:T(8,128)S(1)} %pad_maximum_fusion.one), channel_id=1, source_target_pairs={{0,4},{8,12},{32,36},{40,44},{64,68},{72,76},{96,100},{104,108},{1... | collective-permute-start | bytes 248840 | tf_op jit(solution)/shard_map/ppermute | solution.py:32
  118.2 4.6 %collective-permute-start.19 = (f32[2,81,128]{2,1,0:T(8,128)S(1)}, f32[2,81,128]{2,1,0:T(8,128)S(1)}, u32[]{:S(2)}, u32[]{:S(2)}) collective-permute-start(f32[2,81,128]{2,1,0:T(8,128)S(1)} %pad_maximum_fusion.one), channel_id=1, source_target_pairs={{0,6},{8,14},{32,38},{40,46},{64,70},{72,78},{96,102},{104,110},{1... | collective-permute-start | bytes 248840 | tf_op jit(solution)/shard_map/ppermute | solution.py:32
  122.3 0.6 copy-start.1
  122.3 0.7 copy-start.2
  (1 other events, 0.6 us)
where the time goes:
time: 126 us
  Pallas kernels  43.7 us (35%)
  starting transfers between devices  32.1 us (25%)
  waiting for transfers between devices  27.9 us (22%)
  blocking collectives  13.8 us (11%)
  local copies, waits for them, and re-layouts  3.04 us (2%)
  between operations  2.88 us (2%)
  other arithmetic  2.19 us (2%)
    ppermute x20, starting transfers between devices, moved(): return lax.ppermute(value, AXES, pairs)  32.1 us
    ppermute x20, waiting for transfers between devices, moved(): return lax.ppermute(value, AXES, pairs)  27.9 us
    pallas_call x1, Pallas kernels, arrived_part(): pl.pallas_call(arrived_kernel, out_shape=[jax.ShapeDtypeStruct((D // 4, D...  25.3 us
    all_to_all x1, blocking collectives, local(): three = lax.all_to_all(two, AXES, 0, 0, axis_index_groups=ALONG_Z)  13.8 us
    pallas_call x1, Pallas kernels, own_part(): pl.pallas_call(own_kernel, out_shape=[jax.ShapeDtypeStruct(*result) for r...  11.3 us
    pallas_call x1, Pallas kernels, turn_own(): pl.pallas_call(turn_kernel, out_shape=[jax.ShapeDtypeStruct((D, D), BF16)...  5.07 us
    unnamed x26, local copies, waits for them, and re-layouts  2.79 us
  transfers between devices with their start and end apart: 20, of which 9 were waited for; matrix products, arithmetic and copies ran while one was open for 0% of the time, Pallas kernels for 13%

commit v1 on v0

--- a/solution.py
+++ b/solution.py
@@ -108,18 +108,13 @@
     return waits
 
 
-def project(feats, head, tmp, rows, squares):
-    squares[0:rows] = jnp.zeros((rows, 128), F32)
-
-    @pl.loop(0, 3)
-    def _(k):
-        at = pl.ds(pl.multiple_of(k * 384, 384), 384)
-        p = jnp.dot(feats[0:rows], head[:, at], preferred_element_type=F32)
-        tmp[0:rows, at] = p
-        p = p * p
-        squares[0:rows] += p[:, 0:128] + p[:, 128:256] + p[:, 256:384]
-
-    return lax.rsqrt(jnp.sum(squares[0:rows], axis=1, keepdims=True) + 1e-6)
+def project(feats, head, tmp, rows):
+    squares = jnp.zeros((rows, 1), F32)
+    for n, w in THIRDS:
+        p = jnp.dot(feats[0:rows], head[:, n : n + w], preferred_element_type=F32)
+        tmp[0:rows, n : n + w] = p
+        squares = squares + jnp.sum(p * p, axis=1, keepdims=True)
+    return lax.rsqrt(squares + 1e-6)
 
 
 def one_hot(place_ref, pv):
@@ -156,7 +151,7 @@
 def own_kernel(
     place_ref, sharp_ref, shift_ref, coef_ref, mine_ref, other_ref, im, io, cm, co, wi, wc,
     zx_out, zy_out, ux_out, ix_out, dz_out,
-    f, w, tmp, zx, zy, ux, ix, squares, gs, dz, targets, sems,
+    f, w, tmp, zx, zy, ux, ix, gs, dz, targets, sems,
 ):
     core = place_ref[0]
     first = by_role(
@@ -172,7 +167,7 @@
     targets[1:2, 0:R] = jnp.where(core == 0, other_ref[...], mine_ref[...])
     for wait in first:
         wait.wait()
-    inv = project(f.at[0], w.at[0], tmp, 2 * R, ix)
+    inv = project(f.at[0], w.at[0], tmp, 2 * R)
     ix[...] = jnp.broadcast_to(inv, (2 * R, 128))
     unit = tmp[...] * inv
     ux[...] = unit
@@ -180,7 +175,7 @@
     outs = [fetch(ux, ux_out, sems.at[6]), fetch(zx, zx_out, sems.at[7]), fetch(ix, ix_out, sems.at[8])]
     for wait in second:
         wait.wait()
-    inv = project(f.at[1], w.at[1], tmp, 2 * R, squares)
+    inv = project(f.at[1], w.at[1], tmp, 2 * R)
     for b in range(2):
         zy[b * PAD : b * PAD + R] = (tmp[b * R : (b + 1) * R] * inv[b * R : (b + 1) * R]).astype(BF16)
         zy[b * PAD + R : (b + 1) * PAD] = jnp.zeros((PAD - R, D), BF16)
@@ -228,7 +223,6 @@
             pltpu.VMEM((2 * PAD, D), BF16),
             pltpu.VMEM((2 * R, D), F32),
             pltpu.VMEM((2 * R, 128), F32),
-            pltpu.VMEM((2 * R, 128), F32),
             pltpu.VMEM((2 * R, 2 * PAD), BF16),
             pltpu.VMEM((2 * R, D), F32),
             pltpu.VMEM((2, PAD), jnp.int32),
@@ -301,7 +295,7 @@
     captions.append(fetch(wc, w.at[1], sems.at[6]))
 
     def unit_rows(feats, head, unit, inverse, m, base):
-        inv = project(feats, head, unit, m, inverse)
+        inv = project(feats, head, unit, m)
         inverse[...] = jnp.broadcast_to(inv, (m, 128))
         unit[...] = unit[...] * inv
         z[pl.ds(pl.multiple_of(base, PAD), m)] = unit[...].astype(BF16)
@@ -340,13 +334,11 @@
         copy.wait()
 
     def spread(m, cols, y0, y1, kept, unit, inverse, base):
-        @pl.loop(0, 3)
-        def _(k):
-            at = pl.ds(pl.multiple_of(k * 384, 384), 384)
-            d = scalars[0] * jnp.dot(gs[0:m, 0:cols], z[y0 * PAD : y1 * PAD, at], preferred_element_type=F32)
+        for n, wd in THIRDS:
+            d = scalars[0] * jnp.dot(gs[0:m, 0:cols], z[y0 * PAD : y1 * PAD, n : n + wd], preferred_element_type=F32)
             if kept:
-                d = d + dz[:, at]
-            da[0:m, at] = d
+                d = d + dz[:, n : n + wd]
+            da[0:m, n : n + wd] = d
 
         along = jnp.sum(da[0:m] * unit[0:m], axis=1, keepdims=True)
         dp[base : base + m] = ((da[0:m] - unit[0:m] * along) * inverse[0:m, 0:1]).astype(BF16)

time: 126 us -> 122 us (0.968)
  Pallas kernels: 43.7 us -> 40.9 us
  starting transfers between devices: 32.1 us -> 30.7 us
    pallas_call x1, Pallas kernels: 25.3 us -> 23.3 us  [arrived_part(): pl.pallas_call(arrived_kernel, out_shape=[jax.ShapeDtypeStruct((D // 4, D...]
    ppermute x20, starting transfers between devices: 32.1 us -> 30.7 us  [moved(): return lax.ppermute(value, AXES, pairs)]
  transfers between devices with their start and end apart: 20 -> 20, of which waited for: 9 -> 10; matrix products, arithmetic and copies ran while one was open for 0% -> 1% of each run, Pallas kernels for 13% -> 13%
where the time goes in v1:
time: 122 us
  Pallas kernels  40.9 us (34%)
  starting transfers between devices  30.7 us (25%)
  waiting for transfers between devices  28.7 us (24%)
  blocking collectives  13.7 us (11%)
  local copies, waits for them, and re-layouts  3.04 us (2%)
  between operations  2.87 us (2%)
  other arithmetic  2.19 us (2%)
    ppermute x20, starting transfers between devices, moved(): return lax.ppermute(value, AXES, pairs)  30.7 us
    ppermute x20, waiting for transfers between devices, moved(): return lax.ppermute(value, AXES, pairs)  28.7 us
    pallas_call x1, Pallas kernels, arrived_part(): pl.pallas_call(arrived_kernel, out_shape=[jax.ShapeDtypeStruct((D // 4, D...  23.3 us
    all_to_all x1, blocking collectives, local(): three = lax.all_to_all(two, AXES, 0, 0, axis_index_groups=ALONG_Z)  13.7 us
    pallas_call x1, Pallas kernels, own_part(): pl.pallas_call(own_kernel, out_shape=[jax.ShapeDtypeStruct(*result) for r...  10.5 us
    pallas_call x1, Pallas kernels, turn_own(): pl.pallas_call(turn_kernel, out_shape=[jax.ShapeDtypeStruct((D, D), BF16)...  5.08 us
    unnamed x26, local copies, waits for them, and re-layouts  2.79 us
  transfers between devices with their start and end apart: 20, of which 10 were waited for; matrix products, arithmetic and copies ran while one was open for 1% of the time, Pallas kernels for 13%

profile of v1, /device:TPU:1, one launch (start us, length us, event | category | flops | bytes accessed | tf_op | source)
XLA Modules:
  0.0 122.1 jit_solution(8176718918403742120)
XLA Ops:
  0.6 3.3 %collective-permute-start.4 = (bf16[224,1152]{1,0:T(8,128)(2,1)}, bf16[224,1152]{1,0:T(8,128)(2,1)S(1)}, u32[]{:S(2)}, u32[]{:S(2)}) collective-permute-start(bf16[224,1152]{1,0:T(8,128)(2,1)} %im.2), channel_id=1, source_target_pairs={{0,8},{8,0},{32,40},{40,32},{64,72},{72,64},{96,104},{104,96},{128... | collective-permute-start | bytes 1548296 | tf_op jit(solution)/shard_map/ppermute | solution.py:32
  7.1 3.9 %collective-permute-start.2 = (bf16[224,1152]{1,0:T(8,128)(2,1)}, bf16[224,1152]{1,0:T(8,128)(2,1)S(1)}, u32[]{:S(2)}, u32[]{:S(2)}) collective-permute-start(bf16[224,1152]{1,0:T(8,128)(2,1)} %im.2), channel_id=1, source_target_pairs={{0,224},{8,232},{32,0},{40,8},{64,32},{72,40},{96,64},{104,72},{12... | collective-permute-start | bytes 1548296 | tf_op jit(solution)/shard_map/ppermute | solution.py:32
  11.0 0.7 collective-permute-start.3
  11.8 0.8 copy-done.4
  12.8 10.5 %shard_map.95 = (bf16[448,1152]{1,0:T(8,128)(2,1)}, bf16[512,1152]{1,0:T(8,128)(2,1)}, f32[448,1152]{1,0:T(8,128)}, f32[448,128]{1,0:T(8,128)}, f32[448,1152]{1,0:T(8,128)}) custom-call(s32[4]{0:T(128)} %pad_add_fusion.place_ref, f32[1]{0:T(128)S(6)} %copy.10.sharp_ref, f32[1]{0:T(128)S(6)} %copy.11.shift_ref, f32[1]{0:T(128)S(6)} %div.24.coef_ref, ...), custom_call_target="tpu_custom_call" | custom-call | flops 6000000000 | bytes 16000000 | tf_op jit(solution)/shard_map/pallas_call | solution.py:213
  23.3 0.7 collective-permute-done.1.sm
  24.1 2.6 %collective-permute-start.6 = (bf16[224,1152]{1,0:T(8,128)(2,1)S(1)}, bf16[224,1152]{1,0:T(8,128)(2,1)S(1)}, u32[]{:S(2)}, u32[]{:S(2)}) collective-permute-start(bf16[224,1152]{1,0:T(8,128)(2,1)S(1)} %collective-permute-done.1.sm), channel_id=1, source_target_pairs={{0,8},{8,0},{32,40},{40,32},{64,72},{72,64},{96,104},{104,96},{128... | collective-permute-start | bytes 1548296 | tf_op jit(solution)/shard_map/ppermute | solution.py:32
  27.1 5.1 %shard_map.96 = (bf16[1152,1152]{1,0:T(8,128)(2,1)}, bf16[1152,512]{1,0:T(8,128)(2,1)}) custom-call(s32[4]{0:T(128)} %pad_add_fusion.place_ref, bf16[224,1152]{1,0:T(8,128)(2,1)} %im.2, bf16[224,1152]{1,0:T(8,128)(2,1)} %copy-done.4, bf16[224,1152]{1,0:T(8,128)(2,1)} %cm.2, bf16[224,1152]{1,0:T(8,128)(2,1)} %copy-done.5), custom_call_target="tpu_custom_call" | custom-call | flops 2000000000 | bytes 6000000 | tf_op jit(solution)/shard_map/pallas_call | solution.py:257
  32.3 0.7 copy-done.9
  33.4 23.3 %shard_map.97 = (bf16[288,1152]{1,0:T(8,128)(2,1)}, bf16[288,1152]{1,0:T(8,128)(2,1)}, bf16[288,1152]{1,0:T(8,128)(2,1)}, bf16[288,1152]{1,0:T(8,128)(2,1)}) custom-call(s32[4]{0:T(128)} %pad_add_fusion.place_ref, f32[1]{0:T(128)S(6)} %copy.10.sharp_ref, f32[1]{0:T(128)S(6)} %copy.11.shift_ref, f32[1]{0:T(128)S(6)} %div.24.coef_ref, ...), custom_call_target="tpu_custom_call" | custom-call | flops 14000000000 | bytes 20000000 | tf_op jit(solution)/shard_map/pallas_call | solution.py:388
  56.7 1.3 %collective-permute-start.10 = (bf16[288,1152]{1,0:T(8,128)(2,1)}, bf16[288,1152]{1,0:T(8,128)(2,1)S(1)}, u32[]{:S(2)}, u32[]{:S(2)}) collective-permute-start(bf16[288,1152]{1,0:T(8,128)(2,1)} %get-tuple-element.52), channel_id=1, source_target_pairs={{0,6},{8,25},{32,38},{40,57},{64,70},{72,89},{96,102},{104,121},{1... | collective-permute-start | bytes 1990664 | tf_op jit(solution)/shard_map/ppermute | solution.py:32
  58.0 1.4 %collective-permute-start.11 = (bf16[288,1152]{1,0:T(8,128)(2,1)}, bf16[288,1152]{1,0:T(8,128)(2,1)S(1)}, u32[]{:S(2)}, u32[]{:S(2)}) collective-permute-start(bf16[288,1152]{1,0:T(8,128)(2,1)} %get-tuple-element.53), channel_id=1, source_target_pairs={{0,4},{8,9},{32,36},{40,41},{64,68},{72,73},{96,100},{104,105},{12... | collective-permute-start | bytes 1990664 | tf_op jit(solution)/shard_map/ppermute | solution.py:32
  59.5 0.8 collective-permute-start.9
  60.2 6.5 %collective-permute-done.10 = bf16[288,1152]{1,0:T(8,128)(2,1)S(1)} collective-permute-done((bf16[288,1152]{1,0:T(8,128)(2,1)}, bf16[288,1152]{1,0:T(8,128)(2,1)S(1)}, u32[]{:S(2)}, u32[]{:S(2)}) %collective-permute-start.10) | collective-permute-done | bytes 663584 | tf_op jit(solution)/shard_map/ppermute | solution.py:32
  66.8 2.8 %collective-permute-done.11 = bf16[288,1152]{1,0:T(8,128)(2,1)S(1)} collective-permute-done((bf16[288,1152]{1,0:T(8,128)(2,1)}, bf16[288,1152]{1,0:T(8,128)(2,1)S(1)}, u32[]{:S(2)}, u32[]{:S(2)}) %collective-permute-start.11) | collective-permute-done | bytes 663584 | tf_op jit(solution)/shard_map/ppermute | solution.py:32
  69.6 7.1 %collective-permute-done.9 = bf16[288,1152]{1,0:T(8,128)(2,1)S(1)} collective-permute-done((bf16[288,1152]{1,0:T(8,128)(2,1)}, bf16[288,1152]{1,0:T(8,128)(2,1)S(1)}, u32[]{:S(2)}, u32[]{:S(2)}) %collective-permute-start.9) | collective-permute-done | bytes 663584 | tf_op jit(solution)/shard_map/ppermute | solution.py:32
  76.7 1.4 %add_convert_fusion = bf16[288,1152]{1,0:T(8,128)(2,1)S(1)} fusion(bf16[288,1152]{1,0:T(8,128)(2,1)S(1)} %collective-permute-done.11, bf16[288,1152]{1,0:T(8,128)(2,1)S(1)} %collective-permute-done.10, bf16[288,1152]{1,0:T(8,128)(2,1)S(1)} %collective-permute-done.9, bf16[288,1152]{1,0:T(8,128)(2,1)} %get-tuple-element.50), kind=kLoop, calls=%fused_computation | loop fusion | flops 2654208 | bytes 3317760 | tf_op jit(solution)/shard_map/convert_element_type | solution.py:488
  78.2 1.0 collective-permute-start.12
  79.1 1.8 %collective-permute-start.13 = (bf16[72,1152]{1,0:T(8,128)(2,1)S(1)}, bf16[72,1152]{1,0:T(8,128)(2,1)S(1)}, u32[]{:S(2)}, u32[]{:S(2)}) collective-permute-start(bf16[72,1152]{1,0:T(8,128)(2,1)S(1)} %get-tuple-element.56), channel_id=1, source_target_pairs={{0,17},{8,14},{32,49},{40,46},{64,81},{72,78},{96,113},{104,110},{... | collective-permute-start | bytes 497672 | tf_op jit(solution)/shard_map/ppermute | solution.py:32
  80.9 1.2 %collective-permute-start.14 = (bf16[72,1152]{1,0:T(8,128)(2,1)S(1)}, bf16[72,1152]{1,0:T(8,128)(2,1)S(1)}, u32[]{:S(2)}, u32[]{:S(2)}) collective-permute-start(bf16[72,1152]{1,0:T(8,128)(2,1)S(1)} %get-tuple-element.55), channel_id=1, source_target_pairs={{0,1},{8,12},{32,33},{40,44},{64,65},{72,76},{96,97},{104,108},{12... | collective-permute-start | bytes 497672 | tf_op jit(solution)/shard_map/ppermute | solution.py:32
  82.2 1.5 %collective-permute-done.12 = bf16[72,1152]{1,0:T(8,128)(2,1)S(1)} collective-permute-done((bf16[72,1152]{1,0:T(8,128)(2,1)S(1)}, bf16[72,1152]{1,0:T(8,128)(2,1)S(1)}, u32[]{:S(2)}, u32[]{:S(2)}) %collective-permute-start.12) | collective-permute-done | bytes 165920 | tf_op jit(solution)/shard_map/ppermute | solution.py:32
  83.6 1.3 %collective-permute-done.13 = bf16[72,1152]{1,0:T(8,128)(2,1)S(1)} collective-permute-done((bf16[72,1152]{1,0:T(8,128)(2,1)S(1)}, bf16[72,1152]{1,0:T(8,128)(2,1)S(1)}, u32[]{:S(2)}, u32[]{:S(2)}) %collective-permute-start.13) | collective-permute-done | bytes 165920 | tf_op jit(solution)/shard_map/ppermute | solution.py:32
  85.0 1.6 %collective-permute-done.14 = bf16[72,1152]{1,0:T(8,128)(2,1)S(1)} collective-permute-done((bf16[72,1152]{1,0:T(8,128)(2,1)S(1)}, bf16[72,1152]{1,0:T(8,128)(2,1)S(1)}, u32[]{:S(2)}, u32[]{:S(2)}) %collective-permute-start.14) | collective-permute-done | bytes 165920 | tf_op jit(solution)/shard_map/ppermute | solution.py:32
  86.9 13.7 %all_to_all.5 = bf16[8,81,128]{2,1,0:T(8,128)(2,1)S(1)} all-to-all(bf16[8,81,128]{2,1,0:T(8,128)(2,1)S(1)} %reshape.7), channel_id=1, replica_groups={{0,32,64,96,128,160,192,224},{8,40,72,104,136,168,200,232},{16,48,80,11..., dimensions={0} | all-to-all | bytes 331776 | tf_op jit(solution)/shard_map/all_to_all | solution.py:492
  100.7 5.6 %collective-permute-start.15 = (f32[81,128]{1,0:T(8,128)S(1)}, f32[81,128]{1,0:T(8,128)S(1)}, u32[]{:S(2)}, u32[]{:S(2)}) collective-permute-start(f32[81,128]{1,0:T(8,128)S(1)} %convert_reduce_fusion), channel_id=1, source_target_pairs={{0,1},{8,0},{32,33},{40,32},{64,65},{72,64},{96,97},{104,96},{128,... | collective-permute-start | bytes 124424 | tf_op jit(solution)/shard_map/ppermute | solution.py:32
  106.2 3.2 %collective-permute-start.16 = (f32[81,128]{1,0:T(8,128)S(1)}, f32[81,128]{1,0:T(8,128)S(1)}, u32[]{:S(2)}, u32[]{:S(2)}) collective-permute-start(f32[81,128]{1,0:T(8,128)S(1)} %convert_reduce_fusion), channel_id=1, source_target_pairs={{8,1},{40,33},{72,65},{104,97},{136,129},{168,161},{200,193},{232,... | collective-permute-start | bytes 124424 | tf_op jit(solution)/shard_map/ppermute | solution.py:32
  109.5 3.6 %collective-permute-done.16 = f32[81,128]{1,0:T(8,128)S(1)} collective-permute-done((f32[81,128]{1,0:T(8,128)S(1)}, f32[81,128]{1,0:T(8,128)S(1)}, u32[]{:S(2)}, u32[]{:S(2)}) %collective-permute-start.16) | collective-permute-done | bytes 41504 | tf_op jit(solution)/shard_map/ppermute | solution.py:32
  113.2 1.5 %collective-permute-start.18 = (f32[2,81,128]{2,1,0:T(8,128)S(1)}, f32[2,81,128]{2,1,0:T(8,128)S(1)}, u32[]{:S(2)}, u32[]{:S(2)}) collective-permute-start(f32[2,81,128]{2,1,0:T(8,128)S(1)} %pad_maximum_fusion.one), channel_id=1, source_target_pairs={{0,4},{8,12},{32,36},{40,44},{64,68},{72,76},{96,100},{104,108},{1... | collective-permute-start | bytes 248840 | tf_op jit(solution)/shard_map/ppermute | solution.py:32
  114.7 1.2 collective-permute-start.19
  115.9 2.9 %collective-permute-done.17.two = f32[2,81,128]{2,1,0:T(8,128)S(1)} collective-permute-done((f32[2,81,128]{2,1,0:T(8,128)S(1)}, f32[2,81,128]{2,1,0:T(8,128)S(1)}, u32[]{:S(2)}, u32[]{:S(2)}) %collective-permute-start.17) | collective-permute-done | bytes 82976 | tf_op jit(solution)/shard_map/ppermute | solution.py:32
  119.4 0.6 copy-done.3
  120.1 2.0 %shard_map.98 = (f32[36,1152]{1,0:T(8,128)}, f32[36,1152]{1,0:T(8,128)}) custom-call(s32[4]{0:T(128)} %pad_add_fusion.place_ref, f32[2,81,128]{2,1,0:T(8,128)} %copy-done, f32[2,81,128]{2,1,0:T(8,128)} %copy-done.1, f32[2,81,128]{2,1,0:T(8,128)} %copy-done.2, f32[2,81,128]{2,1,0:T(8,128)} %copy-done.3), custom_call_target="tpu_custom_call" | custom-call | tf_op jit(solution)/shard_map/pallas_call | solution.py:433
  (47 shorter events, 3.5 us)
Async XLA Ops:
  0.6 11.2 %collective-permute-start.4 = (bf16[224,1152]{1,0:T(8,128)(2,1)}, bf16[224,1152]{1,0:T(8,128)(2,1)S(1)}, u32[]{:S(2)}, u32[]{:S(2)}) collective-permute-start(bf16[224,1152]{1,0:T(8,128)(2,1)} %im.2), channel_id=1, source_target_pairs={{0,8},{8,0},{32,40},{40,32},{64,72},{72,64},{96,104},{104,96},{128... | collective-permute-start | bytes 1548296 | tf_op jit(solution)/shard_map/ppermute | solution.py:32
  4.0 7.8 %collective-permute-start.5 = (bf16[224,1152]{1,0:T(8,128)(2,1)}, bf16[224,1152]{1,0:T(8,128)(2,1)S(1)}, u32[]{:S(2)}, u32[]{:S(2)}) collective-permute-start(bf16[224,1152]{1,0:T(8,128)(2,1)} %cm.2), channel_id=1, source_target_pairs={{0,8},{8,0},{32,40},{40,32},{64,72},{72,64},{96,104},{104,96},{128... | collective-permute-start | bytes 1548296 | tf_op jit(solution)/shard_map/ppermute | solution.py:32
  4.1 3.0 %collective-permute-start = (s32[224]{0:T(256)}, s32[224]{0:T(256)S(1)}, u32[]{:S(2)}, u32[]{:S(2)}) collective-permute-start(s32[224]{0:T(256)} %param.12), channel_id=1, source_target_pairs={{0,8},{8,0},{32,40},{40,32},{64,72},{72,64},{96,104},{104,96},{128... | collective-permute-start | bytes 2696 | tf_op jit(solution)/shard_map/ppermute | solution.py:32
  7.0 4.8 %copy-start.12 = (s32[224]{0:T(256)}, s32[224]{0:T(256)S(1)}, u32[]{:S(2)}) copy-start(s32[224]{0:T(256)S(1)} %collective-permute-done) | copy-start | bytes 2692
  7.1 16.3 %collective-permute-start.2 = (bf16[224,1152]{1,0:T(8,128)(2,1)}, bf16[224,1152]{1,0:T(8,128)(2,1)S(1)}, u32[]{:S(2)}, u32[]{:S(2)}) collective-permute-start(bf16[224,1152]{1,0:T(8,128)(2,1)} %im.2), channel_id=1, source_target_pairs={{0,224},{8,232},{32,0},{40,8},{64,32},{72,40},{96,64},{104,72},{12... | collective-permute-start | bytes 1548296 | tf_op jit(solution)/shard_map/ppermute | solution.py:32
  11.0 12.3 %collective-permute-start.3 = (bf16[224,1152]{1,0:T(8,128)(2,1)}, bf16[224,1152]{1,0:T(8,128)(2,1)S(1)}, u32[]{:S(2)}, u32[]{:S(2)}) collective-permute-start(bf16[224,1152]{1,0:T(8,128)(2,1)} %im.2), channel_id=1, source_target_pairs={{16,240},{48,16},{80,48},{112,80},{144,112},{176,144},{208,176},{2... | collective-permute-start | bytes 1548296 | tf_op jit(solution)/shard_map/ppermute | solution.py:32
  11.7 12.4 %collective-permute-start.1 = (bf16[224,1152]{1,0:T(8,128)(2,1)}, bf16[224,1152]{1,0:T(8,128)(2,1)S(1)}, u32[]{:S(2)}, u32[]{:S(2)}) collective-permute-start(bf16[224,1152]{1,0:T(8,128)(2,1)} %cm.2), channel_id=1, source_target_pairs={{0,16},{8,24},{32,48},{40,56},{64,80},{72,88},{96,112},{104,120},{... | collective-permute-start | bytes 1548296 | tf_op jit(solution)/shard_map/ppermute | solution.py:32
  11.8 0.8 copy-start.4
  11.8 1.0 copy-start.5
  23.3 8.9 %copy-start.6 = (bf16[224,1152]{1,0:T(8,128)(2,1)}, bf16[224,1152]{1,0:T(8,128)(2,1)S(1)}, u32[]{:S(2)}) copy-start(bf16[224,1152]{1,0:T(8,128)(2,1)S(1)} %collective-permute-done.2.fm) | copy-start | bytes 1548292
  23.3 8.9 %copy-start.7 = (bf16[224,1152]{1,0:T(8,128)(2,1)}, bf16[224,1152]{1,0:T(8,128)(2,1)S(1)}, u32[]{:S(2)}) copy-start(bf16[224,1152]{1,0:T(8,128)(2,1)S(1)} %collective-permute-done.3.em) | copy-start | bytes 1548292
  24.1 8.2 %copy-start.8 = (bf16[224,1152]{1,0:T(8,128)(2,1)}, bf16[224,1152]{1,0:T(8,128)(2,1)S(1)}, u32[]{:S(2)}) copy-start(bf16[224,1152]{1,0:T(8,128)(2,1)S(1)} %collective-permute-done.1.sm) | copy-start | bytes 1548292
  24.1 8.2 %collective-permute-start.6 = (bf16[224,1152]{1,0:T(8,128)(2,1)S(1)}, bf16[224,1152]{1,0:T(8,128)(2,1)S(1)}, u32[]{:S(2)}, u32[]{:S(2)}) collective-permute-start(bf16[224,1152]{1,0:T(8,128)(2,1)S(1)} %collective-permute-done.1.sm), channel_id=1, source_target_pairs={{0,8},{8,0},{32,40},{40,32},{64,72},{72,64},{96,104},{104,96},{128... | collective-permute-start | bytes 1548296 | tf_op jit(solution)/shard_map/ppermute | solution.py:32
  26.6 5.6 %collective-permute-start.7 = (bf16[224,1152]{1,0:T(8,128)(2,1)S(1)}, bf16[224,1152]{1,0:T(8,128)(2,1)S(1)}, u32[]{:S(2)}, u32[]{:S(2)}) collective-permute-start(bf16[224,1152]{1,0:T(8,128)(2,1)S(1)} %collective-permute-done.2.fm), channel_id=1, source_target_pairs={{0,8},{8,0},{32,40},{40,32},{64,72},{72,64},{96,104},{104,96},{128... | collective-permute-start | bytes 1548296 | tf_op jit(solution)/shard_map/ppermute | solution.py:32
  26.7 5.6 %collective-permute-start.8 = (bf16[224,1152]{1,0:T(8,128)(2,1)S(1)}, bf16[224,1152]{1,0:T(8,128)(2,1)S(1)}, u32[]{:S(2)}, u32[]{:S(2)}) collective-permute-start(bf16[224,1152]{1,0:T(8,128)(2,1)S(1)} %collective-permute-done.3.em), channel_id=1, source_target_pairs={{0,8},{8,0},{32,40},{40,32},{64,72},{72,64},{96,104},{104,96},{128... | collective-permute-start | bytes 1548296 | tf_op jit(solution)/shard_map/ppermute | solution.py:32
  32.3 0.8 copy-start.9
  32.3 1.0 copy-start.10
  32.3 1.1 copy-start.11
  56.7 10.1 %collective-permute-start.10 = (bf16[288,1152]{1,0:T(8,128)(2,1)}, bf16[288,1152]{1,0:T(8,128)(2,1)S(1)}, u32[]{:S(2)}, u32[]{:S(2)}) collective-permute-start(bf16[288,1152]{1,0:T(8,128)(2,1)} %get-tuple-element.52), channel_id=1, source_target_pairs={{0,6},{8,25},{32,38},{40,57},{64,70},{72,89},{96,102},{104,121},{1... | collective-permute-start | bytes 1990664 | tf_op jit(solution)/shard_map/ppermute | solution.py:32
  58.0 11.6 %collective-permute-start.11 = (bf16[288,1152]{1,0:T(8,128)(2,1)}, bf16[288,1152]{1,0:T(8,128)(2,1)S(1)}, u32[]{:S(2)}, u32[]{:S(2)}) collective-permute-start(bf16[288,1152]{1,0:T(8,128)(2,1)} %get-tuple-element.53), channel_id=1, source_target_pairs={{0,4},{8,9},{32,36},{40,41},{64,68},{72,73},{96,100},{104,105},{12... | collective-permute-start | bytes 1990664 | tf_op jit(solution)/shard_map/ppermute | solution.py:32
  59.5 17.2 %collective-permute-start.9 = (bf16[288,1152]{1,0:T(8,128)(2,1)}, bf16[288,1152]{1,0:T(8,128)(2,1)S(1)}, u32[]{:S(2)}, u32[]{:S(2)}) collective-permute-start(bf16[288,1152]{1,0:T(8,128)(2,1)} %get-tuple-element.51), channel_id=1, source_target_pairs={{0,2},{8,24},{32,34},{40,56},{64,66},{72,88},{96,98},{104,120},{12... | collective-permute-start | bytes 1990664 | tf_op jit(solution)/shard_map/ppermute | solution.py:32
  78.2 5.5 %collective-permute-start.12 = (bf16[72,1152]{1,0:T(8,128)(2,1)S(1)}, bf16[72,1152]{1,0:T(8,128)(2,1)S(1)}, u32[]{:S(2)}, u32[]{:S(2)}) collective-permute-start(bf16[72,1152]{1,0:T(8,128)(2,1)S(1)} %get-tuple-element.54), channel_id=1, source_target_pairs={{0,16},{8,10},{32,48},{40,42},{64,80},{72,74},{96,112},{104,106},{... | collective-permute-start | bytes 497672 | tf_op jit(solution)/shard_map/ppermute | solution.py:32
  79.1 5.8 %collective-permute-start.13 = (bf16[72,1152]{1,0:T(8,128)(2,1)S(1)}, bf16[72,1152]{1,0:T(8,128)(2,1)S(1)}, u32[]{:S(2)}, u32[]{:S(2)}) collective-permute-start(bf16[72,1152]{1,0:T(8,128)(2,1)S(1)} %get-tuple-element.56), channel_id=1, source_target_pairs={{0,17},{8,14},{32,49},{40,46},{64,81},{72,78},{96,113},{104,110},{... | collective-permute-start | bytes 497672 | tf_op jit(solution)/shard_map/ppermute | solution.py:32
  80.9 5.7 %collective-permute-start.14 = (bf16[72,1152]{1,0:T(8,128)(2,1)S(1)}, bf16[72,1152]{1,0:T(8,128)(2,1)S(1)}, u32[]{:S(2)}, u32[]{:S(2)}) collective-permute-start(bf16[72,1152]{1,0:T(8,128)(2,1)S(1)} %get-tuple-element.55), channel_id=1, source_target_pairs={{0,1},{8,12},{32,33},{40,44},{64,65},{72,76},{96,97},{104,108},{12... | collective-permute-start | bytes 497672 | tf_op jit(solution)/shard_map/ppermute | solution.py:32
  100.7 8.8 %collective-permute-start.15 = (f32[81,128]{1,0:T(8,128)S(1)}, f32[81,128]{1,0:T(8,128)S(1)}, u32[]{:S(2)}, u32[]{:S(2)}) collective-permute-start(f32[81,128]{1,0:T(8,128)S(1)} %convert_reduce_fusion), channel_id=1, source_target_pairs={{0,1},{8,0},{32,33},{40,32},{64,65},{72,64},{96,97},{104,96},{128,... | collective-permute-start | bytes 124424 | tf_op jit(solution)/shard_map/ppermute | solution.py:32
  106.2 6.9 %collective-permute-start.16 = (f32[81,128]{1,0:T(8,128)S(1)}, f32[81,128]{1,0:T(8,128)S(1)}, u32[]{:S(2)}, u32[]{:S(2)}) collective-permute-start(f32[81,128]{1,0:T(8,128)S(1)} %convert_reduce_fusion), channel_id=1, source_target_pairs={{8,1},{40,33},{72,65},{104,97},{136,129},{168,161},{200,193},{232,... | collective-permute-start | bytes 124424 | tf_op jit(solution)/shard_map/ppermute | solution.py:32
  113.1 6.2 %copy-start = (f32[2,81,128]{2,1,0:T(8,128)}, f32[2,81,128]{2,1,0:T(8,128)S(1)}, u32[]{:S(2)}) copy-start(f32[2,81,128]{2,1,0:T(8,128)S(1)} %pad_maximum_fusion.one) | copy-start | bytes 248836
  113.1 5.6 %collective-permute-start.17 = (f32[2,81,128]{2,1,0:T(8,128)S(1)}, f32[2,81,128]{2,1,0:T(8,128)S(1)}, u32[]{:S(2)}, u32[]{:S(2)}) collective-permute-start(f32[2,81,128]{2,1,0:T(8,128)S(1)} %pad_maximum_fusion.one), channel_id=1, source_target_pairs={{0,2},{8,10},{32,34},{40,42},{64,66},{72,74},{96,98},{104,106},{12... | collective-permute-start | bytes 248840 | tf_op jit(solution)/shard_map/ppermute | solution.py:32
  113.2 5.5 %collective-permute-start.18 = (f32[2,81,128]{2,1,0:T(8,128)S(1)}, f32[2,81,128]{2,1,0:T(8,128)S(1)}, u32[]{:S(2)}, u32[]{:S(2)}) collective-permute-start(f32[2,81,128]{2,1,0:T(8,128)S(1)} %pad_maximum_fusion.one), channel_id=1, source_target_pairs={{0,4},{8,12},{32,36},{40,44},{64,68},{72,76},{96,100},{104,108},{1... | collective-permute-start | bytes 248840 | tf_op jit(solution)/shard_map/ppermute | solution.py:32
  114.7 4.6 %collective-permute-start.19 = (f32[2,81,128]{2,1,0:T(8,128)S(1)}, f32[2,81,128]{2,1,0:T(8,128)S(1)}, u32[]{:S(2)}, u32[]{:S(2)}) collective-permute-start(f32[2,81,128]{2,1,0:T(8,128)S(1)} %pad_maximum_fusion.one), channel_id=1, source_target_pairs={{0,6},{8,14},{32,38},{40,46},{64,70},{72,78},{96,102},{104,110},{1... | collective-permute-start | bytes 248840 | tf_op jit(solution)/shard_map/ppermute | solution.py:32
  118.8 0.6 copy-start.1
  118.8 0.7 copy-start.2
  (1 other events, 0.6 us)

commit v2 on v1

--- a/solution.py
+++ b/solution.py
@@ -416,16 +416,18 @@
     )(place, sharp, shift, coef, *operands)
 
 
-def join_kernel(place_ref, one, two, three, four, image_out, caption_out, held):
+def join_kernel(place_ref, one, two, three, four, image_out, caption_out, held, rows):
     for k, piece in enumerate((one, two, three, four)):
-        held[k] = piece[...]
+        held[k, :, 0:81] = piece[...]
     for place in range(NX):
         back = (place_ref[2] - place) & 3
-        for head, out in enumerate((image_out, caption_out)):
-            for row in range(9):
-                at = place * 9 + row
-                for n in range(9):
-                    out[at : at + 1, n * 128 : (n + 1) * 128] = held[back, head, row * 9 + n : row * 9 + n + 1]
+        for head in range(2):
+            for n in range(9):
+                rows[head, place * 9 : place * 9 + 9, n * 128 : (n + 1) * 128] = held[
+                    back, head, pl.ds(n, 9, stride=9)
+                ]
+    image_out[...] = rows[0, 0:36]
+    caption_out[...] = rows[1, 0:36]
 
 
 def join_rows(place, *pieces):
@@ -435,7 +437,7 @@
         out_shape=[jax.ShapeDtypeStruct((36, D), F32)] * 2,
         in_specs=[pl.BlockSpec(memory_space=pltpu.SMEM)] + [vmem] * 4,
         out_specs=[vmem] * 2,
-        scratch_shapes=[pltpu.VMEM((4, 2, 81, 128), F32)],
+        scratch_shapes=[pltpu.VMEM((4, 2, 144, 128), F32), pltpu.VMEM((2, 48, D), F32)],
     )(place, *pieces)
 
 

time: 122 us -> 122 us (level)
  no operation moved by 1% of the time
where the time goes in v2:
time: 122 us
  Pallas kernels  40.7 us (33%)
  starting transfers between devices  30.7 us (25%)
  waiting for transfers between devices  28.7 us (24%)
  blocking collectives  13.7 us (11%)
  local copies, waits for them, and re-layouts  3.04 us (2%)
  between operations  2.87 us (2%)
  other arithmetic  2.19 us (2%)
    ppermute x20, starting transfers between devices, moved(): return lax.ppermute(value, AXES, pairs)  30.7 us
    ppermute x20, waiting for transfers between devices, moved(): return lax.ppermute(value, AXES, pairs)  28.7 us
    pallas_call x1, Pallas kernels, arrived_part(): pl.pallas_call(arrived_kernel, out_shape=[jax.ShapeDtypeStruct((D // 4, D...  23.3 us
    all_to_all x1, blocking collectives, local(): three = lax.all_to_all(two, AXES, 0, 0, axis_index_groups=ALONG_Z)  13.7 us
    pallas_call x1, Pallas kernels, own_part(): pl.pallas_call(own_kernel, out_shape=[jax.ShapeDtypeStruct(*result) for r...  10.5 us
    pallas_call x1, Pallas kernels, turn_own(): pl.pallas_call(turn_kernel, out_shape=[jax.ShapeDtypeStruct((D, D), BF16)...  5.08 us
    unnamed x26, local copies, waits for them, and re-layouts  2.79 us
  transfers between devices with their start and end apart: 20, of which 10 were waited for; matrix products, arithmetic and copies ran while one was open for 1% of the time, Pallas kernels for 13%

profile of v2, /device:TPU:1, one launch (start us, length us, event | category | flops | bytes accessed | tf_op | source)
XLA Modules:
  0.0 121.9 jit_solution(8772604579437776721)
XLA Ops:
  0.6 3.3 %collective-permute-start.4 = (bf16[224,1152]{1,0:T(8,128)(2,1)}, bf16[224,1152]{1,0:T(8,128)(2,1)S(1)}, u32[]{:S(2)}, u32[]{:S(2)}) collective-permute-start(bf16[224,1152]{1,0:T(8,128)(2,1)} %im.2), channel_id=1, source_target_pairs={{0,8},{8,0},{32,40},{40,32},{64,72},{72,64},{96,104},{104,96},{128... | collective-permute-start | bytes 1548296 | tf_op jit(solution)/shard_map/ppermute | solution.py:32
  7.1 3.9 %collective-permute-start.2 = (bf16[224,1152]{1,0:T(8,128)(2,1)}, bf16[224,1152]{1,0:T(8,128)(2,1)S(1)}, u32[]{:S(2)}, u32[]{:S(2)}) collective-permute-start(bf16[224,1152]{1,0:T(8,128)(2,1)} %im.2), channel_id=1, source_target_pairs={{0,224},{8,232},{32,0},{40,8},{64,32},{72,40},{96,64},{104,72},{12... | collective-permute-start | bytes 1548296 | tf_op jit(solution)/shard_map/ppermute | solution.py:32
  11.0 0.7 collective-permute-start.3
  11.8 0.8 copy-done.4
  12.8 10.5 %shard_map.95 = (bf16[448,1152]{1,0:T(8,128)(2,1)}, bf16[512,1152]{1,0:T(8,128)(2,1)}, f32[448,1152]{1,0:T(8,128)}, f32[448,128]{1,0:T(8,128)}, f32[448,1152]{1,0:T(8,128)}) custom-call(s32[4]{0:T(128)} %pad_add_fusion.place_ref, f32[1]{0:T(128)S(6)} %copy.10.sharp_ref, f32[1]{0:T(128)S(6)} %copy.11.shift_ref, f32[1]{0:T(128)S(6)} %div.24.coef_ref, ...), custom_call_target="tpu_custom_call" | custom-call | flops 6000000000 | bytes 16000000 | tf_op jit(solution)/shard_map/pallas_call | solution.py:213
  23.3 0.7 collective-permute-done.1.sm
  24.1 2.6 %collective-permute-start.6 = (bf16[224,1152]{1,0:T(8,128)(2,1)S(1)}, bf16[224,1152]{1,0:T(8,128)(2,1)S(1)}, u32[]{:S(2)}, u32[]{:S(2)}) collective-permute-start(bf16[224,1152]{1,0:T(8,128)(2,1)S(1)} %collective-permute-done.1.sm), channel_id=1, source_target_pairs={{0,8},{8,0},{32,40},{40,32},{64,72},{72,64},{96,104},{104,96},{128... | collective-permute-start | bytes 1548296 | tf_op jit(solution)/shard_map/ppermute | solution.py:32
  27.1 5.1 %shard_map.96 = (bf16[1152,1152]{1,0:T(8,128)(2,1)}, bf16[1152,512]{1,0:T(8,128)(2,1)}) custom-call(s32[4]{0:T(128)} %pad_add_fusion.place_ref, bf16[224,1152]{1,0:T(8,128)(2,1)} %im.2, bf16[224,1152]{1,0:T(8,128)(2,1)} %copy-done.4, bf16[224,1152]{1,0:T(8,128)(2,1)} %cm.2, bf16[224,1152]{1,0:T(8,128)(2,1)} %copy-done.5), custom_call_target="tpu_custom_call" | custom-call | flops 2000000000 | bytes 6000000 | tf_op jit(solution)/shard_map/pallas_call | solution.py:257
  32.3 0.7 copy-done.9
  33.4 23.3 %shard_map.97 = (bf16[288,1152]{1,0:T(8,128)(2,1)}, bf16[288,1152]{1,0:T(8,128)(2,1)}, bf16[288,1152]{1,0:T(8,128)(2,1)}, bf16[288,1152]{1,0:T(8,128)(2,1)}) custom-call(s32[4]{0:T(128)} %pad_add_fusion.place_ref, f32[1]{0:T(128)S(6)} %copy.10.sharp_ref, f32[1]{0:T(128)S(6)} %copy.11.shift_ref, f32[1]{0:T(128)S(6)} %div.24.coef_ref, ...), custom_call_target="tpu_custom_call" | custom-call | flops 14000000000 | bytes 20000000 | tf_op jit(solution)/shard_map/pallas_call | solution.py:388
  56.7 1.3 %collective-permute-start.10 = (bf16[288,1152]{1,0:T(8,128)(2,1)}, bf16[288,1152]{1,0:T(8,128)(2,1)S(1)}, u32[]{:S(2)}, u32[]{:S(2)}) collective-permute-start(bf16[288,1152]{1,0:T(8,128)(2,1)} %get-tuple-element.52), channel_id=1, source_target_pairs={{0,6},{8,25},{32,38},{40,57},{64,70},{72,89},{96,102},{104,121},{1... | collective-permute-start | bytes 1990664 | tf_op jit(solution)/shard_map/ppermute | solution.py:32
  58.0 1.4 %collective-permute-start.11 = (bf16[288,1152]{1,0:T(8,128)(2,1)}, bf16[288,1152]{1,0:T(8,128)(2,1)S(1)}, u32[]{:S(2)}, u32[]{:S(2)}) collective-permute-start(bf16[288,1152]{1,0:T(8,128)(2,1)} %get-tuple-element.53), channel_id=1, source_target_pairs={{0,4},{8,9},{32,36},{40,41},{64,68},{72,73},{96,100},{104,105},{12... | collective-permute-start | bytes 1990664 | tf_op jit(solution)/shard_map/ppermute | solution.py:32
  59.5 0.8 collective-permute-start.9
  60.2 6.5 %collective-permute-done.10 = bf16[288,1152]{1,0:T(8,128)(2,1)S(1)} collective-permute-done((bf16[288,1152]{1,0:T(8,128)(2,1)}, bf16[288,1152]{1,0:T(8,128)(2,1)S(1)}, u32[]{:S(2)}, u32[]{:S(2)}) %collective-permute-start.10) | collective-permute-done | bytes 663584 | tf_op jit(solution)/shard_map/ppermute | solution.py:32
  66.8 2.8 %collective-permute-done.11 = bf16[288,1152]{1,0:T(8,128)(2,1)S(1)} collective-permute-done((bf16[288,1152]{1,0:T(8,128)(2,1)}, bf16[288,1152]{1,0:T(8,128)(2,1)S(1)}, u32[]{:S(2)}, u32[]{:S(2)}) %collective-permute-start.11) | collective-permute-done | bytes 663584 | tf_op jit(solution)/shard_map/ppermute | solution.py:32
  69.6 7.1 %collective-permute-done.9 = bf16[288,1152]{1,0:T(8,128)(2,1)S(1)} collective-permute-done((bf16[288,1152]{1,0:T(8,128)(2,1)}, bf16[288,1152]{1,0:T(8,128)(2,1)S(1)}, u32[]{:S(2)}, u32[]{:S(2)}) %collective-permute-start.9) | collective-permute-done | bytes 663584 | tf_op jit(solution)/shard_map/ppermute | solution.py:32
  76.7 1.4 %add_convert_fusion = bf16[288,1152]{1,0:T(8,128)(2,1)S(1)} fusion(bf16[288,1152]{1,0:T(8,128)(2,1)S(1)} %collective-permute-done.11, bf16[288,1152]{1,0:T(8,128)(2,1)S(1)} %collective-permute-done.10, bf16[288,1152]{1,0:T(8,128)(2,1)S(1)} %collective-permute-done.9, bf16[288,1152]{1,0:T(8,128)(2,1)} %get-tuple-element.50), kind=kLoop, calls=%fused_computation | loop fusion | flops 2654208 | bytes 3317760 | tf_op jit(solution)/shard_map/convert_element_type | solution.py:490
  78.2 1.0 collective-permute-start.12
  79.1 1.8 %collective-permute-start.13 = (bf16[72,1152]{1,0:T(8,128)(2,1)S(1)}, bf16[72,1152]{1,0:T(8,128)(2,1)S(1)}, u32[]{:S(2)}, u32[]{:S(2)}) collective-permute-start(bf16[72,1152]{1,0:T(8,128)(2,1)S(1)} %get-tuple-element.56), channel_id=1, source_target_pairs={{0,17},{8,14},{32,49},{40,46},{64,81},{72,78},{96,113},{104,110},{... | collective-permute-start | bytes 497672 | tf_op jit(solution)/shard_map/ppermute | solution.py:32
  80.9 1.2 %collective-permute-start.14 = (bf16[72,1152]{1,0:T(8,128)(2,1)S(1)}, bf16[72,1152]{1,0:T(8,128)(2,1)S(1)}, u32[]{:S(2)}, u32[]{:S(2)}) collective-permute-start(bf16[72,1152]{1,0:T(8,128)(2,1)S(1)} %get-tuple-element.55), channel_id=1, source_target_pairs={{0,1},{8,12},{32,33},{40,44},{64,65},{72,76},{96,97},{104,108},{12... | collective-permute-start | bytes 497672 | tf_op jit(solution)/shard_map/ppermute | solution.py:32
  82.2 1.5 %collective-permute-done.12 = bf16[72,1152]{1,0:T(8,128)(2,1)S(1)} collective-permute-done((bf16[72,1152]{1,0:T(8,128)(2,1)S(1)}, bf16[72,1152]{1,0:T(8,128)(2,1)S(1)}, u32[]{:S(2)}, u32[]{:S(2)}) %collective-permute-start.12) | collective-permute-done | bytes 165920 | tf_op jit(solution)/shard_map/ppermute | solution.py:32
  83.6 1.3 %collective-permute-done.13 = bf16[72,1152]{1,0:T(8,128)(2,1)S(1)} collective-permute-done((bf16[72,1152]{1,0:T(8,128)(2,1)S(1)}, bf16[72,1152]{1,0:T(8,128)(2,1)S(1)}, u32[]{:S(2)}, u32[]{:S(2)}) %collective-permute-start.13) | collective-permute-done | bytes 165920 | tf_op jit(solution)/shard_map/ppermute | solution.py:32
  85.0 1.6 %collective-permute-done.14 = bf16[72,1152]{1,0:T(8,128)(2,1)S(1)} collective-permute-done((bf16[72,1152]{1,0:T(8,128)(2,1)S(1)}, bf16[72,1152]{1,0:T(8,128)(2,1)S(1)}, u32[]{:S(2)}, u32[]{:S(2)}) %collective-permute-start.14) | collective-permute-done | bytes 165920 | tf_op jit(solution)/shard_map/ppermute | solution.py:32
  86.9 13.7 %all_to_all.5 = bf16[8,81,128]{2,1,0:T(8,128)(2,1)S(1)} all-to-all(bf16[8,81,128]{2,1,0:T(8,128)(2,1)S(1)} %reshape.7), channel_id=1, replica_groups={{0,32,64,96,128,160,192,224},{8,40,72,104,136,168,200,232},{16,48,80,11..., dimensions={0} | all-to-all | bytes 331776 | tf_op jit(solution)/shard_map/all_to_all | solution.py:494
  100.7 5.6 %collective-permute-start.15 = (f32[81,128]{1,0:T(8,128)S(1)}, f32[81,128]{1,0:T(8,128)S(1)}, u32[]{:S(2)}, u32[]{:S(2)}) collective-permute-start(f32[81,128]{1,0:T(8,128)S(1)} %convert_reduce_fusion), channel_id=1, source_target_pairs={{0,1},{8,0},{32,33},{40,32},{64,65},{72,64},{96,97},{104,96},{128,... | collective-permute-start | bytes 124424 | tf_op jit(solution)/shard_map/ppermute | solution.py:32
  106.2 3.2 %collective-permute-start.16 = (f32[81,128]{1,0:T(8,128)S(1)}, f32[81,128]{1,0:T(8,128)S(1)}, u32[]{:S(2)}, u32[]{:S(2)}) collective-permute-start(f32[81,128]{1,0:T(8,128)S(1)} %convert_reduce_fusion), channel_id=1, source_target_pairs={{8,1},{40,33},{72,65},{104,97},{136,129},{168,161},{200,193},{232,... | collective-permute-start | bytes 124424 | tf_op jit(solution)/shard_map/ppermute | solution.py:32
  109.5 3.6 %collective-permute-done.16 = f32[81,128]{1,0:T(8,128)S(1)} collective-permute-done((f32[81,128]{1,0:T(8,128)S(1)}, f32[81,128]{1,0:T(8,128)S(1)}, u32[]{:S(2)}, u32[]{:S(2)}) %collective-permute-start.16) | collective-permute-done | bytes 41504 | tf_op jit(solution)/shard_map/ppermute | solution.py:32
  113.2 1.5 %collective-permute-start.18 = (f32[2,81,128]{2,1,0:T(8,128)S(1)}, f32[2,81,128]{2,1,0:T(8,128)S(1)}, u32[]{:S(2)}, u32[]{:S(2)}) collective-permute-start(f32[2,81,128]{2,1,0:T(8,128)S(1)} %pad_maximum_fusion.one), channel_id=1, source_target_pairs={{0,4},{8,12},{32,36},{40,44},{64,68},{72,76},{96,100},{104,108},{1... | collective-permute-start | bytes 248840 | tf_op jit(solution)/shard_map/ppermute | solution.py:32
  114.7 1.2 collective-permute-start.19
  115.9 2.9 %collective-permute-done.17.two = f32[2,81,128]{2,1,0:T(8,128)S(1)} collective-permute-done((f32[2,81,128]{2,1,0:T(8,128)S(1)}, f32[2,81,128]{2,1,0:T(8,128)S(1)}, u32[]{:S(2)}, u32[]{:S(2)}) %collective-permute-start.17) | collective-permute-done | bytes 82976 | tf_op jit(solution)/shard_map/ppermute | solution.py:32
  119.4 0.6 copy-done.3
  120.1 1.9 %shard_map.98 = (f32[36,1152]{1,0:T(8,128)}, f32[36,1152]{1,0:T(8,128)}) custom-call(s32[4]{0:T(128)} %pad_add_fusion.place_ref, f32[2,81,128]{2,1,0:T(8,128)} %copy-done, f32[2,81,128]{2,1,0:T(8,128)} %copy-done.1, f32[2,81,128]{2,1,0:T(8,128)} %copy-done.2, f32[2,81,128]{2,1,0:T(8,128)} %copy-done.3), custom_call_target="tpu_custom_call" | custom-call | tf_op jit(solution)/shard_map/pallas_call | solution.py:435
  (47 shorter events, 3.5 us)
Async XLA Ops:
  0.6 11.2 %collective-permute-start.4 = (bf16[224,1152]{1,0:T(8,128)(2,1)}, bf16[224,1152]{1,0:T(8,128)(2,1)S(1)}, u32[]{:S(2)}, u32[]{:S(2)}) collective-permute-start(bf16[224,1152]{1,0:T(8,128)(2,1)} %im.2), channel_id=1, source_target_pairs={{0,8},{8,0},{32,40},{40,32},{64,72},{72,64},{96,104},{104,96},{128... | collective-permute-start | bytes 1548296 | tf_op jit(solution)/shard_map/ppermute | solution.py:32
  4.0 7.8 %collective-permute-start.5 = (bf16[224,1152]{1,0:T(8,128)(2,1)}, bf16[224,1152]{1,0:T(8,128)(2,1)S(1)}, u32[]{:S(2)}, u32[]{:S(2)}) collective-permute-start(bf16[224,1152]{1,0:T(8,128)(2,1)} %cm.2), channel_id=1, source_target_pairs={{0,8},{8,0},{32,40},{40,32},{64,72},{72,64},{96,104},{104,96},{128... | collective-permute-start | bytes 1548296 | tf_op jit(solution)/shard_map/ppermute | solution.py:32
  4.1 3.0 %collective-permute-start = (s32[224]{0:T(256)}, s32[224]{0:T(256)S(1)}, u32[]{:S(2)}, u32[]{:S(2)}) collective-permute-start(s32[224]{0:T(256)} %param.12), channel_id=1, source_target_pairs={{0,8},{8,0},{32,40},{40,32},{64,72},{72,64},{96,104},{104,96},{128... | collective-permute-start | bytes 2696 | tf_op jit(solution)/shard_map/ppermute | solution.py:32
  7.0 4.8 %copy-start.12 = (s32[224]{0:T(256)}, s32[224]{0:T(256)S(1)}, u32[]{:S(2)}) copy-start(s32[224]{0:T(256)S(1)} %collective-permute-done) | copy-start | bytes 2692
  7.1 16.3 %collective-permute-start.2 = (bf16[224,1152]{1,0:T(8,128)(2,1)}, bf16[224,1152]{1,0:T(8,128)(2,1)S(1)}, u32[]{:S(2)}, u32[]{:S(2)}) collective-permute-start(bf16[224,1152]{1,0:T(8,128)(2,1)} %im.2), channel_id=1, source_target_pairs={{0,224},{8,232},{32,0},{40,8},{64,32},{72,40},{96,64},{104,72},{12... | collective-permute-start | bytes 1548296 | tf_op jit(solution)/shard_map/ppermute | solution.py:32
  11.0 12.3 %collective-permute-start.3 = (bf16[224,1152]{1,0:T(8,128)(2,1)}, bf16[224,1152]{1,0:T(8,128)(2,1)S(1)}, u32[]{:S(2)}, u32[]{:S(2)}) collective-permute-start(bf16[224,1152]{1,0:T(8,128)(2,1)} %im.2), channel_id=1, source_target_pairs={{16,240},{48,16},{80,48},{112,80},{144,112},{176,144},{208,176},{2... | collective-permute-start | bytes 1548296 | tf_op jit(solution)/shard_map/ppermute | solution.py:32
  11.7 12.4 %collective-permute-start.1 = (bf16[224,1152]{1,0:T(8,128)(2,1)}, bf16[224,1152]{1,0:T(8,128)(2,1)S(1)}, u32[]{:S(2)}, u32[]{:S(2)}) collective-permute-start(bf16[224,1152]{1,0:T(8,128)(2,1)} %cm.2), channel_id=1, source_target_pairs={{0,16},{8,24},{32,48},{40,56},{64,80},{72,88},{96,112},{104,120},{... | collective-permute-start | bytes 1548296 | tf_op jit(solution)/shard_map/ppermute | solution.py:32
  11.8 0.8 copy-start.4
  11.8 1.0 copy-start.5
  23.3 8.9 %copy-start.6 = (bf16[224,1152]{1,0:T(8,128)(2,1)}, bf16[224,1152]{1,0:T(8,128)(2,1)S(1)}, u32[]{:S(2)}) copy-start(bf16[224,1152]{1,0:T(8,128)(2,1)S(1)} %collective-permute-done.2.fm) | copy-start | bytes 1548292
  23.3 8.9 %copy-start.7 = (bf16[224,1152]{1,0:T(8,128)(2,1)}, bf16[224,1152]{1,0:T(8,128)(2,1)S(1)}, u32[]{:S(2)}) copy-start(bf16[224,1152]{1,0:T(8,128)(2,1)S(1)} %collective-permute-done.3.em) | copy-start | bytes 1548292
  24.1 8.2 %copy-start.8 = (bf16[224,1152]{1,0:T(8,128)(2,1)}, bf16[224,1152]{1,0:T(8,128)(2,1)S(1)}, u32[]{:S(2)}) copy-start(bf16[224,1152]{1,0:T(8,128)(2,1)S(1)} %collective-permute-done.1.sm) | copy-start | bytes 1548292
  24.1 8.2 %collective-permute-start.6 = (bf16[224,1152]{1,0:T(8,128)(2,1)S(1)}, bf16[224,1152]{1,0:T(8,128)(2,1)S(1)}, u32[]{:S(2)}, u32[]{:S(2)}) collective-permute-start(bf16[224,1152]{1,0:T(8,128)(2,1)S(1)} %collective-permute-done.1.sm), channel_id=1, source_target_pairs={{0,8},{8,0},{32,40},{40,32},{64,72},{72,64},{96,104},{104,96},{128... | collective-permute-start | bytes 1548296 | tf_op jit(solution)/shard_map/ppermute | solution.py:32
  26.6 5.6 %collective-permute-start.7 = (bf16[224,1152]{1,0:T(8,128)(2,1)S(1)}, bf16[224,1152]{1,0:T(8,128)(2,1)S(1)}, u32[]{:S(2)}, u32[]{:S(2)}) collective-permute-start(bf16[224,1152]{1,0:T(8,128)(2,1)S(1)} %collective-permute-done.2.fm), channel_id=1, source_target_pairs={{0,8},{8,0},{32,40},{40,32},{64,72},{72,64},{96,104},{104,96},{128... | collective-permute-start | bytes 1548296 | tf_op jit(solution)/shard_map/ppermute | solution.py:32
  26.7 5.6 %collective-permute-start.8 = (bf16[224,1152]{1,0:T(8,128)(2,1)S(1)}, bf16[224,1152]{1,0:T(8,128)(2,1)S(1)}, u32[]{:S(2)}, u32[]{:S(2)}) collective-permute-start(bf16[224,1152]{1,0:T(8,128)(2,1)S(1)} %collective-permute-done.3.em), channel_id=1, source_target_pairs={{0,8},{8,0},{32,40},{40,32},{64,72},{72,64},{96,104},{104,96},{128... | collective-permute-start | bytes 1548296 | tf_op jit(solution)/shard_map/ppermute | solution.py:32
  32.3 0.8 copy-start.9
  32.3 1.0 copy-start.10
  32.3 1.1 copy-start.11
  56.7 10.1 %collective-permute-start.10 = (bf16[288,1152]{1,0:T(8,128)(2,1)}, bf16[288,1152]{1,0:T(8,128)(2,1)S(1)}, u32[]{:S(2)}, u32[]{:S(2)}) collective-permute-start(bf16[288,1152]{1,0:T(8,128)(2,1)} %get-tuple-element.52), channel_id=1, source_target_pairs={{0,6},{8,25},{32,38},{40,57},{64,70},{72,89},{96,102},{104,121},{1... | collective-permute-start | bytes 1990664 | tf_op jit(solution)/shard_map/ppermute | solution.py:32
  58.0 11.6 %collective-permute-start.11 = (bf16[288,1152]{1,0:T(8,128)(2,1)}, bf16[288,1152]{1,0:T(8,128)(2,1)S(1)}, u32[]{:S(2)}, u32[]{:S(2)}) collective-permute-start(bf16[288,1152]{1,0:T(8,128)(2,1)} %get-tuple-element.53), channel_id=1, source_target_pairs={{0,4},{8,9},{32,36},{40,41},{64,68},{72,73},{96,100},{104,105},{12... | collective-permute-start | bytes 1990664 | tf_op jit(solution)/shard_map/ppermute | solution.py:32
  59.5 17.2 %collective-permute-start.9 = (bf16[288,1152]{1,0:T(8,128)(2,1)}, bf16[288,1152]{1,0:T(8,128)(2,1)S(1)}, u32[]{:S(2)}, u32[]{:S(2)}) collective-permute-start(bf16[288,1152]{1,0:T(8,128)(2,1)} %get-tuple-element.51), channel_id=1, source_target_pairs={{0,2},{8,24},{32,34},{40,56},{64,66},{72,88},{96,98},{104,120},{12... | collective-permute-start | bytes 1990664 | tf_op jit(solution)/shard_map/ppermute | solution.py:32
  78.2 5.5 %collective-permute-start.12 = (bf16[72,1152]{1,0:T(8,128)(2,1)S(1)}, bf16[72,1152]{1,0:T(8,128)(2,1)S(1)}, u32[]{:S(2)}, u32[]{:S(2)}) collective-permute-start(bf16[72,1152]{1,0:T(8,128)(2,1)S(1)} %get-tuple-element.54), channel_id=1, source_target_pairs={{0,16},{8,10},{32,48},{40,42},{64,80},{72,74},{96,112},{104,106},{... | collective-permute-start | bytes 497672 | tf_op jit(solution)/shard_map/ppermute | solution.py:32
  79.1 5.8 %collective-permute-start.13 = (bf16[72,1152]{1,0:T(8,128)(2,1)S(1)}, bf16[72,1152]{1,0:T(8,128)(2,1)S(1)}, u32[]{:S(2)}, u32[]{:S(2)}) collective-permute-start(bf16[72,1152]{1,0:T(8,128)(2,1)S(1)} %get-tuple-element.56), channel_id=1, source_target_pairs={{0,17},{8,14},{32,49},{40,46},{64,81},{72,78},{96,113},{104,110},{... | collective-permute-start | bytes 497672 | tf_op jit(solution)/shard_map/ppermute | solution.py:32
  80.9 5.7 %collective-permute-start.14 = (bf16[72,1152]{1,0:T(8,128)(2,1)S(1)}, bf16[72,1152]{1,0:T(8,128)(2,1)S(1)}, u32[]{:S(2)}, u32[]{:S(2)}) collective-permute-start(bf16[72,1152]{1,0:T(8,128)(2,1)S(1)} %get-tuple-element.55), channel_id=1, source_target_pairs={{0,1},{8,12},{32,33},{40,44},{64,65},{72,76},{96,97},{104,108},{12... | collective-permute-start | bytes 497672 | tf_op jit(solution)/shard_map/ppermute | solution.py:32
  100.7 8.8 %collective-permute-start.15 = (f32[81,128]{1,0:T(8,128)S(1)}, f32[81,128]{1,0:T(8,128)S(1)}, u32[]{:S(2)}, u32[]{:S(2)}) collective-permute-start(f32[81,128]{1,0:T(8,128)S(1)} %convert_reduce_fusion), channel_id=1, source_target_pairs={{0,1},{8,0},{32,33},{40,32},{64,65},{72,64},{96,97},{104,96},{128,... | collective-permute-start | bytes 124424 | tf_op jit(solution)/shard_map/ppermute | solution.py:32
  106.2 6.9 %collective-permute-start.16 = (f32[81,128]{1,0:T(8,128)S(1)}, f32[81,128]{1,0:T(8,128)S(1)}, u32[]{:S(2)}, u32[]{:S(2)}) collective-permute-start(f32[81,128]{1,0:T(8,128)S(1)} %convert_reduce_fusion), channel_id=1, source_target_pairs={{8,1},{40,33},{72,65},{104,97},{136,129},{168,161},{200,193},{232,... | collective-permute-start | bytes 124424 | tf_op jit(solution)/shard_map/ppermute | solution.py:32
  113.1 6.2 %copy-start = (f32[2,81,128]{2,1,0:T(8,128)}, f32[2,81,128]{2,1,0:T(8,128)S(1)}, u32[]{:S(2)}) copy-start(f32[2,81,128]{2,1,0:T(8,128)S(1)} %pad_maximum_fusion.one) | copy-start | bytes 248836
  113.1 5.6 %collective-permute-start.17 = (f32[2,81,128]{2,1,0:T(8,128)S(1)}, f32[2,81,128]{2,1,0:T(8,128)S(1)}, u32[]{:S(2)}, u32[]{:S(2)}) collective-permute-start(f32[2,81,128]{2,1,0:T(8,128)S(1)} %pad_maximum_fusion.one), channel_id=1, source_target_pairs={{0,2},{8,10},{32,34},{40,42},{64,66},{72,74},{96,98},{104,106},{12... | collective-permute-start | bytes 248840 | tf_op jit(solution)/shard_map/ppermute | solution.py:32
  113.2 5.5 %collective-permute-start.18 = (f32[2,81,128]{2,1,0:T(8,128)S(1)}, f32[2,81,128]{2,1,0:T(8,128)S(1)}, u32[]{:S(2)}, u32[]{:S(2)}) collective-permute-start(f32[2,81,128]{2,1,0:T(8,128)S(1)} %pad_maximum_fusion.one), channel_id=1, source_target_pairs={{0,4},{8,12},{32,36},{40,44},{64,68},{72,76},{96,100},{104,108},{1... | collective-permute-start | bytes 248840 | tf_op jit(solution)/shard_map/ppermute | solution.py:32
  114.7 4.6 %collective-permute-start.19 = (f32[2,81,128]{2,1,0:T(8,128)S(1)}, f32[2,81,128]{2,1,0:T(8,128)S(1)}, u32[]{:S(2)}, u32[]{:S(2)}) collective-permute-start(f32[2,81,128]{2,1,0:T(8,128)S(1)} %pad_maximum_fusion.one), channel_id=1, source_target_pairs={{0,6},{8,14},{32,38},{40,46},{64,70},{72,78},{96,102},{104,110},{1... | collective-permute-start | bytes 248840 | tf_op jit(solution)/shard_map/ppermute | solution.py:32
  118.8 0.6 copy-start.1
  118.8 0.7 copy-start.2
  (1 other events, 0.6 us)

commit v3 on v1

--- a/solution.py
+++ b/solution.py
@@ -191,7 +191,7 @@
     scalars = (sharp_ref[0], shift_ref[0])
     pair_weights(scalars, zx[...], zy[...], (0, 1), R, (0, 1), lambda x, y: coef_ref[0], gs, label)
 
-    @pl.loop(0, 3)
+    @pl.loop(0, 3, unroll=3)
     def _(k):
         cols = pl.ds(pl.multiple_of(k * 384, 384), 384)
         dz[:, cols] = sharp_ref[0] * jnp.dot(gs[...], zy[:, cols], preferred_element_type=F32)
@@ -242,7 +242,7 @@
     for wait in feats:
         wait.wait()
 
-    @pl.loop(0, 3)
+    @pl.loop(0, 3, unroll=3)
     def _(k):
         rows = pl.ds(pl.multiple_of(k * 384, 384), 384)
         ft[rows, 0 : 2 * R] = nt_dot(pv[rows], f[...]).astype(BF16)

time: 122 us -> 121 us (level)
  transfers between devices with their start and end apart: 20 -> 20, of which waited for: 10 -> 9; matrix products, arithmetic and copies ran while one was open for 1% -> 1% of each run, Pallas kernels for 13% -> 12%
where the time goes in v3:
time: 121 us
  Pallas kernels  39.9 us (33%)
  starting transfers between devices  30.5 us (25%)
  waiting for transfers between devices  29.5 us (24%)
  blocking collectives  13.1 us (11%)
  local copies, waits for them, and re-layouts  3.04 us (3%)
  between operations  2.87 us (2%)
  other arithmetic  2.19 us (2%)
    ppermute x20, starting transfers between devices, moved(): return lax.ppermute(value, AXES, pairs)  30.5 us
    ppermute x20, waiting for transfers between devices, moved(): return lax.ppermute(value, AXES, pairs)  29.5 us
    pallas_call x1, Pallas kernels, arrived_part(): pl.pallas_call(arrived_kernel, out_shape=[jax.ShapeDtypeStruct((D // 4, D...  23.3 us
    all_to_all x1, blocking collectives, local(): three = lax.all_to_all(two, AXES, 0, 0, axis_index_groups=ALONG_Z)  13.1 us
    pallas_call x1, Pallas kernels, own_part(): pl.pallas_call(own_kernel, out_shape=[jax.ShapeDtypeStruct(*result) for r...  9.96 us
    pallas_call x1, Pallas kernels, turn_own(): pl.pallas_call(turn_kernel, out_shape=[jax.ShapeDtypeStruct((D, D), BF16)...  4.65 us
    unnamed x26, local copies, waits for them, and re-layouts  2.79 us
  transfers between devices with their start and end apart: 20, of which 9 were waited for; matrix products, arithmetic and copies ran while one was open for 1% of the time, Pallas kernels for 12%

profile of v3, /device:TPU:1, one launch (start us, length us, event | category | flops | bytes accessed | tf_op | source)
XLA Modules:
  0.0 121.1 jit_solution(3824487160121243941)
XLA Ops:
  0.6 3.3 %collective-permute-start.4 = (bf16[224,1152]{1,0:T(8,128)(2,1)}, bf16[224,1152]{1,0:T(8,128)(2,1)S(1)}, u32[]{:S(2)}, u32[]{:S(2)}) collective-permute-start(bf16[224,1152]{1,0:T(8,128)(2,1)} %im.2), channel_id=1, source_target_pairs={{0,8},{8,0},{32,40},{40,32},{64,72},{72,64},{96,104},{104,96},{128... | collective-permute-start | bytes 1548296 | tf_op jit(solution)/shard_map/ppermute | solution.py:32
  4.5 0.6 pad_add_fusion.place_ref
  7.1 3.9 %collective-permute-start.2 = (bf16[224,1152]{1,0:T(8,128)(2,1)}, bf16[224,1152]{1,0:T(8,128)(2,1)S(1)}, u32[]{:S(2)}, u32[]{:S(2)}) collective-permute-start(bf16[224,1152]{1,0:T(8,128)(2,1)} %im.2), channel_id=1, source_target_pairs={{0,224},{8,232},{32,0},{40,8},{64,32},{72,40},{96,64},{104,72},{12... | collective-permute-start | bytes 1548296 | tf_op jit(solution)/shard_map/ppermute | solution.py:32
  11.0 0.7 collective-permute-start.3
  11.8 0.8 copy-done.4
  12.8 10.0 %shard_map.95 = (bf16[448,1152]{1,0:T(8,128)(2,1)}, bf16[512,1152]{1,0:T(8,128)(2,1)}, f32[448,1152]{1,0:T(8,128)}, f32[448,128]{1,0:T(8,128)}, f32[448,1152]{1,0:T(8,128)}) custom-call(s32[4]{0:T(128)} %pad_add_fusion.place_ref, f32[1]{0:T(128)S(6)} %copy.10.sharp_ref, f32[1]{0:T(128)S(6)} %copy.11.shift_ref, f32[1]{0:T(128)S(6)} %div.24.coef_ref, ...), custom_call_target="tpu_custom_call" | custom-call | flops 6000000000 | bytes 16000000 | tf_op jit(solution)/shard_map/pallas_call | solution.py:213
  22.8 1.3 %collective-permute-done.1.sm = bf16[224,1152]{1,0:T(8,128)(2,1)S(1)} collective-permute-done((bf16[224,1152]{1,0:T(8,128)(2,1)}, bf16[224,1152]{1,0:T(8,128)(2,1)S(1)}, u32[]{:S(2)}, u32[]{:S(2)}) %collective-permute-start.1) | collective-permute-done | bytes 516128 | tf_op jit(solution)/shard_map/ppermute | solution.py:32
  24.1 2.1 %collective-permute-start.6 = (bf16[224,1152]{1,0:T(8,128)(2,1)S(1)}, bf16[224,1152]{1,0:T(8,128)(2,1)S(1)}, u32[]{:S(2)}, u32[]{:S(2)}) collective-permute-start(bf16[224,1152]{1,0:T(8,128)(2,1)S(1)} %collective-permute-done.1.sm), channel_id=1, source_target_pairs={{0,8},{8,0},{32,40},{40,32},{64,72},{72,64},{96,104},{104,96},{128... | collective-permute-start | bytes 1548296 | tf_op jit(solution)/shard_map/ppermute | solution.py:32
  26.7 4.7 %shard_map.96 = (bf16[1152,1152]{1,0:T(8,128)(2,1)}, bf16[1152,512]{1,0:T(8,128)(2,1)}) custom-call(s32[4]{0:T(128)} %pad_add_fusion.place_ref, bf16[224,1152]{1,0:T(8,128)(2,1)} %im.2, bf16[224,1152]{1,0:T(8,128)(2,1)} %copy-done.4, bf16[224,1152]{1,0:T(8,128)(2,1)} %cm.2, bf16[224,1152]{1,0:T(8,128)(2,1)} %copy-done.5), custom_call_target="tpu_custom_call" | custom-call | flops 2000000000 | bytes 6000000 | tf_op jit(solution)/shard_map/pallas_call | solution.py:257
  31.4 0.7 copy-done.9
  32.5 23.3 %shard_map.97 = (bf16[288,1152]{1,0:T(8,128)(2,1)}, bf16[288,1152]{1,0:T(8,128)(2,1)}, bf16[288,1152]{1,0:T(8,128)(2,1)}, bf16[288,1152]{1,0:T(8,128)(2,1)}) custom-call(s32[4]{0:T(128)} %pad_add_fusion.place_ref, f32[1]{0:T(128)S(6)} %copy.10.sharp_ref, f32[1]{0:T(128)S(6)} %copy.11.shift_ref, f32[1]{0:T(128)S(6)} %div.24.coef_ref, ...), custom_call_target="tpu_custom_call" | custom-call | flops 14000000000 | bytes 20000000 | tf_op jit(solution)/shard_map/pallas_call | solution.py:388
  55.8 1.8 %collective-permute-start.10 = (bf16[288,1152]{1,0:T(8,128)(2,1)}, bf16[288,1152]{1,0:T(8,128)(2,1)S(1)}, u32[]{:S(2)}, u32[]{:S(2)}) collective-permute-start(bf16[288,1152]{1,0:T(8,128)(2,1)} %get-tuple-element.52), channel_id=1, source_target_pairs={{0,6},{8,25},{32,38},{40,57},{64,70},{72,89},{96,102},{104,121},{1... | collective-permute-start | bytes 1990664 | tf_op jit(solution)/shard_map/ppermute | solution.py:32
  57.6 1.3 %collective-permute-start.11 = (bf16[288,1152]{1,0:T(8,128)(2,1)}, bf16[288,1152]{1,0:T(8,128)(2,1)S(1)}, u32[]{:S(2)}, u32[]{:S(2)}) collective-permute-start(bf16[288,1152]{1,0:T(8,128)(2,1)} %get-tuple-element.53), channel_id=1, source_target_pairs={{0,4},{8,9},{32,36},{40,41},{64,68},{72,73},{96,100},{104,105},{12... | collective-permute-start | bytes 1990664 | tf_op jit(solution)/shard_map/ppermute | solution.py:32
  58.9 0.8 collective-permute-start.9
  59.6 13.0 %collective-permute-done.10 = bf16[288,1152]{1,0:T(8,128)(2,1)S(1)} collective-permute-done((bf16[288,1152]{1,0:T(8,128)(2,1)}, bf16[288,1152]{1,0:T(8,128)(2,1)S(1)}, u32[]{:S(2)}, u32[]{:S(2)}) %collective-permute-start.10) | collective-permute-done | bytes 663584 | tf_op jit(solution)/shard_map/ppermute | solution.py:32
  72.7 3.6 %collective-permute-done.9 = bf16[288,1152]{1,0:T(8,128)(2,1)S(1)} collective-permute-done((bf16[288,1152]{1,0:T(8,128)(2,1)}, bf16[288,1152]{1,0:T(8,128)(2,1)S(1)}, u32[]{:S(2)}, u32[]{:S(2)}) %collective-permute-start.9) | collective-permute-done | bytes 663584 | tf_op jit(solution)/shard_map/ppermute | solution.py:32
  76.3 1.4 %add_convert_fusion = bf16[288,1152]{1,0:T(8,128)(2,1)S(1)} fusion(bf16[288,1152]{1,0:T(8,128)(2,1)S(1)} %collective-permute-done.11, bf16[288,1152]{1,0:T(8,128)(2,1)S(1)} %collective-permute-done.10, bf16[288,1152]{1,0:T(8,128)(2,1)S(1)} %collective-permute-done.9, bf16[288,1152]{1,0:T(8,128)(2,1)} %get-tuple-element.50), kind=kLoop, calls=%fused_computation | loop fusion | flops 2654208 | bytes 3317760 | tf_op jit(solution)/shard_map/convert_element_type | solution.py:488
  77.7 1.0 collective-permute-start.12
  78.7 1.8 %collective-permute-start.13 = (bf16[72,1152]{1,0:T(8,128)(2,1)S(1)}, bf16[72,1152]{1,0:T(8,128)(2,1)S(1)}, u32[]{:S(2)}, u32[]{:S(2)}) collective-permute-start(bf16[72,1152]{1,0:T(8,128)(2,1)S(1)} %get-tuple-element.56), channel_id=1, source_target_pairs={{0,17},{8,14},{32,49},{40,46},{64,81},{72,78},{96,113},{104,110},{... | collective-permute-start | bytes 497672 | tf_op jit(solution)/shard_map/ppermute | solution.py:32
  80.5 1.2 %collective-permute-start.14 = (bf16[72,1152]{1,0:T(8,128)(2,1)S(1)}, bf16[72,1152]{1,0:T(8,128)(2,1)S(1)}, u32[]{:S(2)}, u32[]{:S(2)}) collective-permute-start(bf16[72,1152]{1,0:T(8,128)(2,1)S(1)} %get-tuple-element.55), channel_id=1, source_target_pairs={{0,1},{8,12},{32,33},{40,44},{64,65},{72,76},{96,97},{104,108},{12... | collective-permute-start | bytes 497672 | tf_op jit(solution)/shard_map/ppermute | solution.py:32
  81.7 1.5 %collective-permute-done.12 = bf16[72,1152]{1,0:T(8,128)(2,1)S(1)} collective-permute-done((bf16[72,1152]{1,0:T(8,128)(2,1)S(1)}, bf16[72,1152]{1,0:T(8,128)(2,1)S(1)}, u32[]{:S(2)}, u32[]{:S(2)}) %collective-permute-start.12) | collective-permute-done | bytes 165920 | tf_op jit(solution)/shard_map/ppermute | solution.py:32
  83.2 1.3 %collective-permute-done.13 = bf16[72,1152]{1,0:T(8,128)(2,1)S(1)} collective-permute-done((bf16[72,1152]{1,0:T(8,128)(2,1)S(1)}, bf16[72,1152]{1,0:T(8,128)(2,1)S(1)}, u32[]{:S(2)}, u32[]{:S(2)}) %collective-permute-start.13) | collective-permute-done | bytes 165920 | tf_op jit(solution)/shard_map/ppermute | solution.py:32
  84.6 1.6 %collective-permute-done.14 = bf16[72,1152]{1,0:T(8,128)(2,1)S(1)} collective-permute-done((bf16[72,1152]{1,0:T(8,128)(2,1)S(1)}, bf16[72,1152]{1,0:T(8,128)(2,1)S(1)}, u32[]{:S(2)}, u32[]{:S(2)}) %collective-permute-start.14) | collective-permute-done | bytes 165920 | tf_op jit(solution)/shard_map/ppermute | solution.py:32
  86.5 13.1 %all_to_all.5 = bf16[8,81,128]{2,1,0:T(8,128)(2,1)S(1)} all-to-all(bf16[8,81,128]{2,1,0:T(8,128)(2,1)S(1)} %reshape.7), channel_id=1, replica_groups={{0,32,64,96,128,160,192,224},{8,40,72,104,136,168,200,232},{16,48,80,11..., dimensions={0} | all-to-all | bytes 331776 | tf_op jit(solution)/shard_map/all_to_all | solution.py:492
  99.7 5.6 %collective-permute-start.15 = (f32[81,128]{1,0:T(8,128)S(1)}, f32[81,128]{1,0:T(8,128)S(1)}, u32[]{:S(2)}, u32[]{:S(2)}) collective-permute-start(f32[81,128]{1,0:T(8,128)S(1)} %convert_reduce_fusion), channel_id=1, source_target_pairs={{0,1},{8,0},{32,33},{40,32},{64,65},{72,64},{96,97},{104,96},{128,... | collective-permute-start | bytes 124424 | tf_op jit(solution)/shard_map/ppermute | solution.py:32
  105.2 3.2 %collective-permute-start.16 = (f32[81,128]{1,0:T(8,128)S(1)}, f32[81,128]{1,0:T(8,128)S(1)}, u32[]{:S(2)}, u32[]{:S(2)}) collective-permute-start(f32[81,128]{1,0:T(8,128)S(1)} %convert_reduce_fusion), channel_id=1, source_target_pairs={{8,1},{40,33},{72,65},{104,97},{136,129},{168,161},{200,193},{232,... | collective-permute-start | bytes 124424 | tf_op jit(solution)/shard_map/ppermute | solution.py:32
  108.5 3.6 %collective-permute-done.16 = f32[81,128]{1,0:T(8,128)S(1)} collective-permute-done((f32[81,128]{1,0:T(8,128)S(1)}, f32[81,128]{1,0:T(8,128)S(1)}, u32[]{:S(2)}, u32[]{:S(2)}) %collective-permute-start.16) | collective-permute-done | bytes 41504 | tf_op jit(solution)/shard_map/ppermute | solution.py:32
  112.2 1.5 %collective-permute-start.18 = (f32[2,81,128]{2,1,0:T(8,128)S(1)}, f32[2,81,128]{2,1,0:T(8,128)S(1)}, u32[]{:S(2)}, u32[]{:S(2)}) collective-permute-start(f32[2,81,128]{2,1,0:T(8,128)S(1)} %pad_maximum_fusion.one), channel_id=1, source_target_pairs={{0,4},{8,12},{32,36},{40,44},{64,68},{72,76},{96,100},{104,108},{1... | collective-permute-start | bytes 248840 | tf_op jit(solution)/shard_map/ppermute | solution.py:32
  113.7 1.2 collective-permute-start.19
  114.9 2.9 %collective-permute-done.17.two = f32[2,81,128]{2,1,0:T(8,128)S(1)} collective-permute-done((f32[2,81,128]{2,1,0:T(8,128)S(1)}, f32[2,81,128]{2,1,0:T(8,128)S(1)}, u32[]{:S(2)}, u32[]{:S(2)}) %collective-permute-start.17) | collective-permute-done | bytes 82976 | tf_op jit(solution)/shard_map/ppermute | solution.py:32
  118.4 0.6 copy-done.3
  119.1 2.0 %shard_map.98 = (f32[36,1152]{1,0:T(8,128)}, f32[36,1152]{1,0:T(8,128)}) custom-call(s32[4]{0:T(128)} %pad_add_fusion.place_ref, f32[2,81,128]{2,1,0:T(8,128)} %copy-done, f32[2,81,128]{2,1,0:T(8,128)} %copy-done.1, f32[2,81,128]{2,1,0:T(8,128)} %copy-done.2, f32[2,81,128]{2,1,0:T(8,128)} %copy-done.3), custom_call_target="tpu_custom_call" | custom-call | tf_op jit(solution)/shard_map/pallas_call | solution.py:433
  (47 shorter events, 2.9 us)
Async XLA Ops:
  0.6 11.2 %collective-permute-start.4 = (bf16[224,1152]{1,0:T(8,128)(2,1)}, bf16[224,1152]{1,0:T(8,128)(2,1)S(1)}, u32[]{:S(2)}, u32[]{:S(2)}) collective-permute-start(bf16[224,1152]{1,0:T(8,128)(2,1)} %im.2), channel_id=1, source_target_pairs={{0,8},{8,0},{32,40},{40,32},{64,72},{72,64},{96,104},{104,96},{128... | collective-permute-start | bytes 1548296 | tf_op jit(solution)/shard_map/ppermute | solution.py:32
  4.0 7.8 %collective-permute-start.5 = (bf16[224,1152]{1,0:T(8,128)(2,1)}, bf16[224,1152]{1,0:T(8,128)(2,1)S(1)}, u32[]{:S(2)}, u32[]{:S(2)}) collective-permute-start(bf16[224,1152]{1,0:T(8,128)(2,1)} %cm.2), channel_id=1, source_target_pairs={{0,8},{8,0},{32,40},{40,32},{64,72},{72,64},{96,104},{104,96},{128... | collective-permute-start | bytes 1548296 | tf_op jit(solution)/shard_map/ppermute | solution.py:32
  4.1 3.0 %collective-permute-start = (s32[224]{0:T(256)}, s32[224]{0:T(256)S(1)}, u32[]{:S(2)}, u32[]{:S(2)}) collective-permute-start(s32[224]{0:T(256)} %param.12), channel_id=1, source_target_pairs={{0,8},{8,0},{32,40},{40,32},{64,72},{72,64},{96,104},{104,96},{128... | collective-permute-start | bytes 2696 | tf_op jit(solution)/shard_map/ppermute | solution.py:32
  7.0 4.8 %copy-start.12 = (s32[224]{0:T(256)}, s32[224]{0:T(256)S(1)}, u32[]{:S(2)}) copy-start(s32[224]{0:T(256)S(1)} %collective-permute-done) | copy-start | bytes 2692
  7.1 15.7 %collective-permute-start.2 = (bf16[224,1152]{1,0:T(8,128)(2,1)}, bf16[224,1152]{1,0:T(8,128)(2,1)S(1)}, u32[]{:S(2)}, u32[]{:S(2)}) collective-permute-start(bf16[224,1152]{1,0:T(8,128)(2,1)} %im.2), channel_id=1, source_target_pairs={{0,224},{8,232},{32,0},{40,8},{64,32},{72,40},{96,64},{104,72},{12... | collective-permute-start | bytes 1548296 | tf_op jit(solution)/shard_map/ppermute | solution.py:32
  11.0 11.8 %collective-permute-start.3 = (bf16[224,1152]{1,0:T(8,128)(2,1)}, bf16[224,1152]{1,0:T(8,128)(2,1)S(1)}, u32[]{:S(2)}, u32[]{:S(2)}) collective-permute-start(bf16[224,1152]{1,0:T(8,128)(2,1)} %im.2), channel_id=1, source_target_pairs={{16,240},{48,16},{80,48},{112,80},{144,112},{176,144},{208,176},{2... | collective-permute-start | bytes 1548296 | tf_op jit(solution)/shard_map/ppermute | solution.py:32
  11.7 12.4 %collective-permute-start.1 = (bf16[224,1152]{1,0:T(8,128)(2,1)}, bf16[224,1152]{1,0:T(8,128)(2,1)S(1)}, u32[]{:S(2)}, u32[]{:S(2)}) collective-permute-start(bf16[224,1152]{1,0:T(8,128)(2,1)} %cm.2), channel_id=1, source_target_pairs={{0,16},{8,24},{32,48},{40,56},{64,80},{72,88},{96,112},{104,120},{... | collective-permute-start | bytes 1548296 | tf_op jit(solution)/shard_map/ppermute | solution.py:32
  11.8 0.8 copy-start.4
  11.8 1.0 copy-start.5
  22.7 8.6 %copy-start.6 = (bf16[224,1152]{1,0:T(8,128)(2,1)}, bf16[224,1152]{1,0:T(8,128)(2,1)S(1)}, u32[]{:S(2)}) copy-start(bf16[224,1152]{1,0:T(8,128)(2,1)S(1)} %collective-permute-done.2.fm) | copy-start | bytes 1548292
  22.8 8.6 %copy-start.7 = (bf16[224,1152]{1,0:T(8,128)(2,1)}, bf16[224,1152]{1,0:T(8,128)(2,1)S(1)}, u32[]{:S(2)}) copy-start(bf16[224,1152]{1,0:T(8,128)(2,1)S(1)} %collective-permute-done.3.em) | copy-start | bytes 1548292
  24.1 7.3 %copy-start.8 = (bf16[224,1152]{1,0:T(8,128)(2,1)}, bf16[224,1152]{1,0:T(8,128)(2,1)S(1)}, u32[]{:S(2)}) copy-start(bf16[224,1152]{1,0:T(8,128)(2,1)S(1)} %collective-permute-done.1.sm) | copy-start | bytes 1548292
  24.1 7.3 %collective-permute-start.6 = (bf16[224,1152]{1,0:T(8,128)(2,1)S(1)}, bf16[224,1152]{1,0:T(8,128)(2,1)S(1)}, u32[]{:S(2)}, u32[]{:S(2)}) collective-permute-start(bf16[224,1152]{1,0:T(8,128)(2,1)S(1)} %collective-permute-done.1.sm), channel_id=1, source_target_pairs={{0,8},{8,0},{32,40},{40,32},{64,72},{72,64},{96,104},{104,96},{128... | collective-permute-start | bytes 1548296 | tf_op jit(solution)/shard_map/ppermute | solution.py:32
  26.1 5.2 %collective-permute-start.7 = (bf16[224,1152]{1,0:T(8,128)(2,1)S(1)}, bf16[224,1152]{1,0:T(8,128)(2,1)S(1)}, u32[]{:S(2)}, u32[]{:S(2)}) collective-permute-start(bf16[224,1152]{1,0:T(8,128)(2,1)S(1)} %collective-permute-done.2.fm), channel_id=1, source_target_pairs={{0,8},{8,0},{32,40},{40,32},{64,72},{72,64},{96,104},{104,96},{128... | collective-permute-start | bytes 1548296 | tf_op jit(solution)/shard_map/ppermute | solution.py:32
  26.1 5.2 %collective-permute-start.8 = (bf16[224,1152]{1,0:T(8,128)(2,1)S(1)}, bf16[224,1152]{1,0:T(8,128)(2,1)S(1)}, u32[]{:S(2)}, u32[]{:S(2)}) collective-permute-start(bf16[224,1152]{1,0:T(8,128)(2,1)S(1)} %collective-permute-done.3.em), channel_id=1, source_target_pairs={{0,8},{8,0},{32,40},{40,32},{64,72},{72,64},{96,104},{104,96},{128... | collective-permute-start | bytes 1548296 | tf_op jit(solution)/shard_map/ppermute | solution.py:32
  31.4 0.8 copy-start.9
  31.4 1.0 copy-start.10
  31.4 1.1 copy-start.11
  55.8 16.9 %collective-permute-start.10 = (bf16[288,1152]{1,0:T(8,128)(2,1)}, bf16[288,1152]{1,0:T(8,128)(2,1)S(1)}, u32[]{:S(2)}, u32[]{:S(2)}) collective-permute-start(bf16[288,1152]{1,0:T(8,128)(2,1)} %get-tuple-element.52), channel_id=1, source_target_pairs={{0,6},{8,25},{32,38},{40,57},{64,70},{72,89},{96,102},{104,121},{1... | collective-permute-start | bytes 1990664 | tf_op jit(solution)/shard_map/ppermute | solution.py:32
  57.6 15.1 %collective-permute-start.11 = (bf16[288,1152]{1,0:T(8,128)(2,1)}, bf16[288,1152]{1,0:T(8,128)(2,1)S(1)}, u32[]{:S(2)}, u32[]{:S(2)}) collective-permute-start(bf16[288,1152]{1,0:T(8,128)(2,1)} %get-tuple-element.53), channel_id=1, source_target_pairs={{0,4},{8,9},{32,36},{40,41},{64,68},{72,73},{96,100},{104,105},{12... | collective-permute-start | bytes 1990664 | tf_op jit(solution)/shard_map/ppermute | solution.py:32
  58.9 17.4 %collective-permute-start.9 = (bf16[288,1152]{1,0:T(8,128)(2,1)}, bf16[288,1152]{1,0:T(8,128)(2,1)S(1)}, u32[]{:S(2)}, u32[]{:S(2)}) collective-permute-start(bf16[288,1152]{1,0:T(8,128)(2,1)} %get-tuple-element.51), channel_id=1, source_target_pairs={{0,2},{8,24},{32,34},{40,56},{64,66},{72,88},{96,98},{104,120},{12... | collective-permute-start | bytes 1990664 | tf_op jit(solution)/shard_map/ppermute | solution.py:32
  77.7 5.5 %collective-permute-start.12 = (bf16[72,1152]{1,0:T(8,128)(2,1)S(1)}, bf16[72,1152]{1,0:T(8,128)(2,1)S(1)}, u32[]{:S(2)}, u32[]{:S(2)}) collective-permute-start(bf16[72,1152]{1,0:T(8,128)(2,1)S(1)} %get-tuple-element.54), channel_id=1, source_target_pairs={{0,16},{8,10},{32,48},{40,42},{64,80},{72,74},{96,112},{104,106},{... | collective-permute-start | bytes 497672 | tf_op jit(solution)/shard_map/ppermute | solution.py:32
  78.7 5.8 %collective-permute-start.13 = (bf16[72,1152]{1,0:T(8,128)(2,1)S(1)}, bf16[72,1152]{1,0:T(8,128)(2,1)S(1)}, u32[]{:S(2)}, u32[]{:S(2)}) collective-permute-start(bf16[72,1152]{1,0:T(8,128)(2,1)S(1)} %get-tuple-element.56), channel_id=1, source_target_pairs={{0,17},{8,14},{32,49},{40,46},{64,81},{72,78},{96,113},{104,110},{... | collective-permute-start | bytes 497672 | tf_op jit(solution)/shard_map/ppermute | solution.py:32
  80.5 5.7 %collective-permute-start.14 = (bf16[72,1152]{1,0:T(8,128)(2,1)S(1)}, bf16[72,1152]{1,0:T(8,128)(2,1)S(1)}, u32[]{:S(2)}, u32[]{:S(2)}) collective-permute-start(bf16[72,1152]{1,0:T(8,128)(2,1)S(1)} %get-tuple-element.55), channel_id=1, source_target_pairs={{0,1},{8,12},{32,33},{40,44},{64,65},{72,76},{96,97},{104,108},{12... | collective-permute-start | bytes 497672 | tf_op jit(solution)/shard_map/ppermute | solution.py:32
  99.7 8.8 %collective-permute-start.15 = (f32[81,128]{1,0:T(8,128)S(1)}, f32[81,128]{1,0:T(8,128)S(1)}, u32[]{:S(2)}, u32[]{:S(2)}) collective-permute-start(f32[81,128]{1,0:T(8,128)S(1)} %convert_reduce_fusion), channel_id=1, source_target_pairs={{0,1},{8,0},{32,33},{40,32},{64,65},{72,64},{96,97},{104,96},{128,... | collective-permute-start | bytes 124424 | tf_op jit(solution)/shard_map/ppermute | solution.py:32
  105.2 6.9 %collective-permute-start.16 = (f32[81,128]{1,0:T(8,128)S(1)}, f32[81,128]{1,0:T(8,128)S(1)}, u32[]{:S(2)}, u32[]{:S(2)}) collective-permute-start(f32[81,128]{1,0:T(8,128)S(1)} %convert_reduce_fusion), channel_id=1, source_target_pairs={{8,1},{40,33},{72,65},{104,97},{136,129},{168,161},{200,193},{232,... | collective-permute-start | bytes 124424 | tf_op jit(solution)/shard_map/ppermute | solution.py:32
  112.1 6.2 %copy-start = (f32[2,81,128]{2,1,0:T(8,128)}, f32[2,81,128]{2,1,0:T(8,128)S(1)}, u32[]{:S(2)}) copy-start(f32[2,81,128]{2,1,0:T(8,128)S(1)} %pad_maximum_fusion.one) | copy-start | bytes 248836
  112.1 5.6 %collective-permute-start.17 = (f32[2,81,128]{2,1,0:T(8,128)S(1)}, f32[2,81,128]{2,1,0:T(8,128)S(1)}, u32[]{:S(2)}, u32[]{:S(2)}) collective-permute-start(f32[2,81,128]{2,1,0:T(8,128)S(1)} %pad_maximum_fusion.one), channel_id=1, source_target_pairs={{0,2},{8,10},{32,34},{40,42},{64,66},{72,74},{96,98},{104,106},{12... | collective-permute-start | bytes 248840 | tf_op jit(solution)/shard_map/ppermute | solution.py:32
  112.2 5.5 %collective-permute-start.18 = (f32[2,81,128]{2,1,0:T(8,128)S(1)}, f32[2,81,128]{2,1,0:T(8,128)S(1)}, u32[]{:S(2)}, u32[]{:S(2)}) collective-permute-start(f32[2,81,128]{2,1,0:T(8,128)S(1)} %pad_maximum_fusion.one), channel_id=1, source_target_pairs={{0,4},{8,12},{32,36},{40,44},{64,68},{72,76},{96,100},{104,108},{1... | collective-permute-start | bytes 248840 | tf_op jit(solution)/shard_map/ppermute | solution.py:32
  113.7 4.6 %collective-permute-start.19 = (f32[2,81,128]{2,1,0:T(8,128)S(1)}, f32[2,81,128]{2,1,0:T(8,128)S(1)}, u32[]{:S(2)}, u32[]{:S(2)}) collective-permute-start(f32[2,81,128]{2,1,0:T(8,128)S(1)} %pad_maximum_fusion.one), channel_id=1, source_target_pairs={{0,6},{8,14},{32,38},{40,46},{64,70},{72,78},{96,102},{104,110},{1... | collective-permute-start | bytes 248840 | tf_op jit(solution)/shard_map/ppermute | solution.py:32
  117.8 0.6 copy-start.1
  117.8 0.7 copy-start.2
  (1 other events, 0.6 us)
